TPU v7x, 32 devices: a whole 2x2x4 slice. The times are simulated.
32 devices in a mesh: rows: 8 (over y, x, core), cols: 4 (over z).
Axes of the slice: x: 2, y: 2, z: 4, core: 2. Of those that a mesh axis runs over, the one named last changes fastest.
Arguments:
- tokens: bfloat16 [32768, 1024], P('rows', 'cols'), may hold values from -6 to 6
- qkv_weight: bfloat16 [1024, 4096], P('rows', 'cols'), may hold values from -0.1875 to 0.1875
- out_weight: bfloat16 [2048, 1024], P('cols', 'rows'), may hold values from -1 to 1
- expand_weight: bfloat16 [1024, 2, 3072], P('rows', None, 'cols'), may hold values from -0.1875 to 0.1875
- down_weight: bfloat16 [3072, 1024], P('cols', 'rows'), may hold values from -0.109375 to 0.109375
- attn_gain: float32 [1024], replicated, may hold values from 0.1 to 1.9
- mlp_gain: float32 [1024], replicated, may hold values from 0.1 to 1.9
- query_gain: float32 [128], replicated, may hold values from 0.1 to 1.9
- key_gain: float32 [128], replicated, may hold values from 0.1 to 1.9
- segment_ids: int32 [8, 4096], P('rows'), may hold values from 0 to 3, never falling along the last dimension, each value on 1 to 2048 neighbouring positions
- cotangent: bfloat16 [32768, 1024], P('rows', 'cols'), may hold values from -6 to 6
Outputs:
- output: bfloat16 [32768, 1024], P('rows', 'cols')
- input_grad: float32 [32768, 1024], P('rows', 'cols')
- qkv_grad: float32 [1024, 4096], P('rows', 'cols')
- out_grad: float32 [2048, 1024], P('cols', 'rows')
- expand_grad: float32 [1024, 2, 3072], P('rows', None, 'cols')
- down_grad: float32 [3072, 1024], P('cols', 'rows')
- attn_gain_grad: float32 [1024], replicated
- mlp_gain_grad: float32 [1024], replicated
- query_gain_grad: float32 [128], replicated
- key_gain_grad: float32 [128], replicated
Inputs may be any that keep to these rules, and one draw needn't show every extreme that they name: `segment_ids`: within a sequence the document numbers never fall, every number from 0 to 3 appears, each document has at most 2048 tokens and one has exactly that many.
All inputs are finite; a program needn't handle non-finite values.
Results may differ from a plain program's by a relative error of at most 0.013.
Values may be sent and summed in bfloat16 or wider, within the bound.
A program may use at most 512 MiB of HBM per device.

v0:
```python
from functools import partial

import jax
import jax.numpy as jnp
from jax import lax
from jax.sharding import PartitionSpec as P

D = 1024
HEADS = 16
KV_HEADS = 8
HEAD = 128
DOCS = 4


EPS = 1e-06
THETA = 1000000.0


def feature_total(values):
    return lax.psum(jnp.sum(values, axis=1), "cols")


def gather_features(values):
    return lax.all_gather(values, "cols", axis=1, tiled=True)


def scatter_features(partial_sum):
    return lax.psum_scatter(partial_sum, "cols", scatter_dimension=1, tiled=True)


def norm_scale(values):
    return lax.rsqrt(feature_total(values * values) / D + EPS)[:, None]


def norm_backward(values, scale, scaling, gradient):
    inner_sum = feature_total(gradient * scaling * values)[:, None]
    back_grad = scale * scaling * gradient - values * scale * scale * scale * inner_sum / D
    gain_part = jnp.sum(gradient * values * scale, axis=0)
    return (back_grad, gain_part)


def project_in(gathered, weight):
    return jnp.einsum(
        "tk,ksf->tsf",
        gathered,
        lax.all_gather(weight, "rows", axis=0, tiled=True),
        preferred_element_type=jnp.float32,
    )


def back_in(gradient, weight):
    return jnp.einsum(
        "tsf,ksf->tk",
        gradient,
        lax.all_gather(weight, "rows", axis=0, tiled=True),
        preferred_element_type=jnp.float32,
    )


def grads_in(gathered, gradient):
    return lax.psum_scatter(
        jnp.einsum("tk,tsf->ksf", gathered, gradient, preferred_element_type=jnp.float32),
        "rows",
        scatter_dimension=0,
        tiled=True,
    )


def project_out(values, weight):
    return jnp.dot(
        values,
        lax.all_gather(weight, "rows", axis=1, tiled=True),
        preferred_element_type=jnp.float32,
    )


def back_out(gathered, weight):
    contract = (((1,), (1,)), ((), ()))
    return lax.dot_general(
        gathered,
        lax.all_gather(weight, "rows", axis=1, tiled=True),
        contract,
        preferred_element_type=jnp.float32,
    )


def grads_out(values, gathered):
    term_part = lax.dot_general(
        values, gathered, (((0,), (0,)), ((), ())), preferred_element_type=jnp.float32
    )
    return lax.psum_scatter(term_part, "rows", scatter_dimension=1, tiled=True)


def rotate(values, cosine, sine_table):
    half_size = values.shape[-1] // 2
    front = values[..., :half_size]
    back_half = values[..., half_size:]
    return jnp.concatenate(
        [front * cosine - back_half * sine_table, back_half * cosine + front * sine_table], axis=-1
    )


def head_norm(values, scaling):
    return values * lax.rsqrt(jnp.mean(values * values, axis=-1, keepdims=True) + EPS) * scaling


def rope_tables(segment):
    length = segment.shape[0]
    member = segment[:, None] == jnp.arange(DOCS, dtype=jnp.int32)[None, :]
    doc_sizes = jnp.sum(member.astype(jnp.int32), axis=0, dtype=jnp.int32)
    starts = jnp.cumsum(doc_sizes, dtype=jnp.int32) - doc_sizes
    doc_start = jnp.sum(jnp.where(member, starts[None, :], 0), axis=1, dtype=jnp.int32)
    position = (jnp.arange(length, dtype=jnp.int32) - doc_start).astype(jnp.float32)
    frequency = THETA ** (-jnp.arange(0, HEAD, 2, dtype=jnp.float32) / HEAD)
    angles = position[:, None] * frequency[None, :]
    return (jnp.cos(angles), jnp.sin(angles))


def heads_local(query_raw, key_raw, query_gain, key_gain, cosine, sine_table):
    queries = rotate(
        head_norm(query_raw, query_gain), cosine[:, None, None], sine_table[:, None, None]
    )
    keys = rotate(head_norm(key_raw, key_gain), cosine[:, None], sine_table[:, None])
    return (queries, keys)


def block_scores(queries, keys, segment, begin_at, end_at):
    scale = queries.shape[-1] ** (-0.5)
    places = jnp.arange(end_at, dtype=jnp.int32)
    scores = (
        jnp.einsum(
            "qhgd,khd->hgqk",
            queries[begin_at:end_at],
            keys[:end_at],
            preferred_element_type=jnp.float32,
        )
        * scale
    )
    allowed = (segment[begin_at:end_at, None] == segment[None, :end_at]) & (
        places[begin_at:end_at, None] >= places[None, :]
    )
    return jnp.where(allowed, scores, -1e30)


def attend(queries, keys, values, segment):
    length = queries.shape[0]
    block_rows = min(512, length)
    outputs = []
    logsums = []
    for begin_at in range(0, length, block_rows):
        end_at = begin_at + block_rows
        scores = block_scores(queries, keys, segment, begin_at, end_at)
        peak = jnp.max(scores, axis=-1, keepdims=True)
        weights = jnp.exp(scores - peak)
        row_sum = jnp.sum(weights, axis=-1, keepdims=True)
        chances = (weights / row_sum).astype(jnp.bfloat16)
        outputs.append(
            jnp.einsum(
                "hgqk,khd->qhgd", chances, values[:end_at], preferred_element_type=jnp.float32
            )
        )
        logsums.append(peak + jnp.log(row_sum))
    return (jnp.concatenate(outputs, axis=0), jnp.concatenate(logsums, axis=2))


def attend_back(queries, keys, values, segment, logsums, grad_mixed):
    length = queries.shape[0]
    block_rows = min(512, length)
    scale = queries.shape[-1] ** (-0.5)
    query_grads = []
    key_grad = jnp.zeros(keys.shape, jnp.float32)
    value_grad = jnp.zeros(values.shape, jnp.float32)
    for begin_at in range(0, length, block_rows):
        end_at = begin_at + block_rows
        scores = block_scores(queries, keys, segment, begin_at, end_at)
        chances = jnp.exp(scores - logsums[:, :, begin_at:end_at])
        grad_block = grad_mixed[begin_at:end_at]
        chance_grad = jnp.einsum(
            "qhgd,khd->hgqk", grad_block, values[:end_at], preferred_element_type=jnp.float32
        )
        value_grad = value_grad.at[:end_at].add(
            jnp.einsum(
                "hgqk,qhgd->khd",
                chances.astype(jnp.bfloat16),
                grad_block,
                preferred_element_type=jnp.float32,
            )
        )
        inner_sum = jnp.sum(chances * chance_grad, axis=-1, keepdims=True)
        score_grad = (chances * (chance_grad - inner_sum)).astype(jnp.bfloat16)
        query_grads.append(
            jnp.einsum(
                "hgqk,khd->qhgd", score_grad, keys[:end_at], preferred_element_type=jnp.float32
            )
            * scale
        )
        key_grad = key_grad.at[:end_at].add(
            jnp.einsum(
                "hgqk,qhgd->khd",
                score_grad,
                queries[begin_at:end_at],
                preferred_element_type=jnp.float32,
            )
            * scale
        )
    return (jnp.concatenate(query_grads, axis=0), key_grad, value_grad)


def attention_output(mixed, out_weight):
    return scatter_features(project_out(mixed, out_weight))


def local(
    tokens,
    qkv_weight,
    out_weight,
    expand_weight,
    down_weight,
    attn_gain,
    mlp_gain,
    query_gain,
    key_gain,
    segment_ids,
    cotangent,
):
    inputs_local = tokens.astype(jnp.float32)
    segment = segment_ids[0]
    length = inputs_local.shape[0]
    local_width = inputs_local.shape[1]
    per_group = HEADS // KV_HEADS
    offset = lax.axis_index("cols") * local_width
    gain_one = lax.dynamic_slice_in_dim(attn_gain, offset, local_width)
    gain_two = lax.dynamic_slice_in_dim(mlp_gain, offset, local_width)
    cosine, sine_table = rope_tables(segment)
    scale_one = norm_scale(inputs_local)
    gathered_one = gather_features((inputs_local * scale_one * gain_one).astype(jnp.bfloat16))
    qkv_local = qkv_weight.reshape(qkv_weight.shape[0], 1, qkv_weight.shape[1])
    projected = project_in(gathered_one, qkv_local)
    groups = projected.shape[-1] // ((per_group + 2) * HEAD)
    grouped = projected.reshape(length, groups, per_group + 2, HEAD)
    query_raw = grouped[:, :, :per_group]
    key_raw = grouped[:, :, per_group]
    queries_f, keys_f = heads_local(query_raw, key_raw, query_gain, key_gain, cosine, sine_table)
    queries = queries_f.astype(jnp.bfloat16)
    keys = keys_f.astype(jnp.bfloat16)
    values = grouped[:, :, per_group + 1].astype(jnp.bfloat16)
    mixed_f, logsums = attend(queries, keys, values, segment)
    mixed = mixed_f.astype(jnp.bfloat16).reshape(length, groups * per_group * HEAD)
    hidden = inputs_local + attention_output(mixed, out_weight)
    scale_two = norm_scale(hidden)
    gathered_two = gather_features((hidden * scale_two * gain_two).astype(jnp.bfloat16))
    gate_up = project_in(gathered_two, expand_weight)
    gate = gate_up[:, 0]
    upper = gate_up[:, 1]
    sigmoid_gate = jax.nn.sigmoid(gate)
    silu_gate = gate * sigmoid_gate
    activation = (silu_gate * upper).astype(jnp.bfloat16)
    mlp_part = project_out(activation, down_weight)
    result = hidden + scatter_features(mlp_part)
    output = result.astype(jnp.bfloat16)
    gradient = cotangent.astype(jnp.float32)
    grad_gathered = gather_features(cotangent)
    act_grad = back_out(grad_gathered, down_weight)
    down_grad = grads_out(activation, grad_gathered)
    gate_grad = act_grad * upper * sigmoid_gate * (1.0 + gate * (1.0 - sigmoid_gate))
    upper_grad = act_grad * silu_gate
    expand_back = jnp.stack([gate_grad, upper_grad], axis=1).astype(jnp.bfloat16)
    normed_grad_two = scatter_features(back_in(expand_back, expand_weight))
    expand_grad = grads_in(gathered_two, expand_back)
    back_two, gain_two_grad = norm_backward(hidden, scale_two, gain_two, normed_grad_two)
    hidden_grad = gradient + back_two
    hidden_gathered = gather_features(hidden_grad.astype(jnp.bfloat16))
    mixed_grad = (
        back_out(hidden_gathered, out_weight)
        .astype(jnp.bfloat16)
        .reshape(length, groups, per_group, HEAD)
    )
    out_grad = grads_out(mixed, hidden_gathered)
    query_grad, key_grad, value_grad = attend_back(
        queries, keys, values, segment, logsums, mixed_grad
    )
    local_heads = partial(heads_local, cosine=cosine, sine_table=sine_table)
    unused_out, pullback = jax.vjp(local_heads, query_raw, key_raw, query_gain, key_gain)
    query_raw_grad, key_raw_grad, query_gain_part, key_gain_part = pullback((query_grad, key_grad))
    qkv_back = jnp.concatenate(
        [query_raw_grad, key_raw_grad[:, :, None], value_grad[:, :, None]], axis=2
    )
    qkv_back = qkv_back.reshape(length, 1, groups * (per_group + 2) * HEAD).astype(jnp.bfloat16)
    normed_grad_one = scatter_features(back_in(qkv_back, qkv_local))
    qkv_grad = grads_in(gathered_one, qkv_back).reshape(qkv_weight.shape)
    back_one, gain_one_grad = norm_backward(inputs_local, scale_one, gain_one, normed_grad_one)
    input_grad = hidden_grad + back_one
    zero_gain = jnp.zeros((D,), jnp.float32)
    attn_gain_part = lax.dynamic_update_slice_in_dim(zero_gain, gain_one_grad, offset, 0)
    mlp_gain_part = lax.dynamic_update_slice_in_dim(zero_gain, gain_two_grad, offset, 0)
    attn_gain_grad, mlp_gain_grad, query_gain_grad, key_gain_grad = lax.psum(
        (attn_gain_part, mlp_gain_part, query_gain_part, key_gain_part), ("rows", "cols")
    )
    return (
        output,
        input_grad,
        qkv_grad,
        out_grad,
        expand_grad,
        down_grad,
        attn_gain_grad,
        mlp_gain_grad,
        query_gain_grad,
        key_gain_grad,
    )


def solution(mesh):
    return jax.shard_map(
        local,
        mesh=mesh,
        in_specs=(
            P("rows", "cols"),
            P("rows", "cols"),
            P("cols", "rows"),
            P("rows", None, "cols"),
            P("cols", "rows"),
            P(),
            P(),
            P(),
            P(),
            P("rows", None),
            P("rows", "cols"),
        ),
        out_specs=(
            P("rows", "cols"),
            P("rows", "cols"),
            P("rows", "cols"),
            P("cols", "rows"),
            P("rows", None, "cols"),
            P("cols", "rows"),
            P(),
            P(),
            P(),
            P(),
        ),
        check_vma=False,
    )
```

profile of v0, /device:TPU:0, one launch (start us, length us, event | category | flops | bytes accessed | tf_op | source)
XLA Modules:
  0.0 2790.6 jit_solution(14777624632134663059)
XLA Ops:
  11.0 20.5 psum.56
  61.3 130.6 %all-gather.10.cloned.1.call-done = bf16[4096,1024]{1,0:T(8,128)(2,1)} async-done(((bf16[4096,256]{1,0:T(8,128)(2,1)}), bf16[4096,1024]{1,0:T(8,128)(2,1)}) %all-gather.10.cloned.1.call-update) | async-done | bytes 8388624 | tf_op jit(solution)/shard_map/all_gather | solution.py:24
  191.8 14.5 fusion.304
  328.8 13.9 fusion.310
  342.6 11.7 fusion.7
  354.9 13.0 fusion.225
  367.9 15.3 fusion.311
  383.3 13.0 fusion.3
  396.4 14.4 fusion.226
  433.9 12.9 fusion.312
  449.6 275.8 %reduce-scatter.9.cloned.1.call-done = f32[4096,256]{1,0:T(8,128)} async-done(((f32[4096,1024]{1,0:T(8,128)}), f32[4096,256]{1,0:T(8,128)}) %reduce-scatter.9.cloned.1.call-update) | async-done | bytes 4194320 | tf_op jit(solution)/shard_map/reduce_scatter | solution.py:28
  730.1 18.2 psum.57
  753.9 150.7 %all-gather.20.cloned.1.call-done = bf16[4096,1024]{1,0:T(8,128)(2,1)} async-done(((bf16[4096,256]{1,0:T(8,128)(2,1)}), bf16[4096,1024]{1,0:T(8,128)(2,1)}) %all-gather.20.cloned.1.call-update) | async-done | bytes 8388624 | tf_op jit(solution)/shard_map/all_gather | solution.py:24
  904.6 12.4 fusion.314
  917.1 20.7 all-gather.16.cloned.1.call-done
  937.8 151.4 %all-gather.14.cloned.1.call-done = bf16[4096,1024]{1,0:T(8,128)(2,1)} async-done(((bf16[4096,256]{1,0:T(8,128)(2,1)}), bf16[4096,1024]{1,0:T(8,128)(2,1)}) %all-gather.14.cloned.1.call-update) | async-done | bytes 8388624 | tf_op jit(solution)/shard_map/all_gather | solution.py:24
  1089.2 21.3 fusion.56
  1110.4 19.1 fusion.70
  1129.5 19.3 convolution_bitcast_fusion
  1150.2 13.0 fusion.313
  1163.3 264.1 %reduce-scatter.13.cloned.1.call-done = f32[4096,256]{1,0:T(8,128)} async-done(((f32[4096,1024]{1,0:T(8,128)}), f32[4096,256]{1,0:T(8,128)}) %reduce-scatter.13.cloned.1.call-update) | async-done | bytes 4194320 | tf_op jit(solution)/shard_map/reduce_scatter | solution.py:28
  1432.2 18.7 psum.58
  1451.0 260.1 %reduce-scatter.11.cloned.1.call-done = f32[4096,256]{1,0:T(8,128)} async-done(((f32[4096,1024]{1,0:T(8,128)}), f32[4096,256]{1,0:T(8,128)}) %reduce-scatter.11.cloned.1.call-update) | async-done | bytes 4194320 | tf_op jit(solution)/shard_map/reduce_scatter | solution.py:28
  1721.4 19.8 fusion.54
  1741.2 127.4 %all-gather.22.cloned.1.call-done = bf16[4096,1024]{1,0:T(8,128)(2,1)} async-done(((bf16[4096,256]{1,0:T(8,128)(2,1)}), bf16[4096,1024]{1,0:T(8,128)(2,1)}) %all-gather.22.cloned.1.call-update) | async-done | bytes 8388624 | tf_op jit(solution)/shard_map/all_gather | solution.py:24
  1923.9 13.4 fusion.37
  1982.1 13.7 fusion.14
  1995.8 20.5 fusion.16
  2032.3 17.0 fusion.9
  2049.3 23.3 fusion.11
  2091.0 20.5 fusion.4
  2111.5 25.0 fusion.6
  2136.6 13.1 fusion.82
  2158.3 23.0 fusion
  2181.3 28.2 %fusion.2 = bf16[2,2,512,4096]{2,3,1,0:T(8,128)(2,1)} fusion(f32[2,4096,512,2]{2,1,3,0:T(8,128)} %get-tuple-element.317, f32[2,2,512,4096]{2,3,1,0:T(8,128)} %get-tuple-element.301, f32[2,2,512]{2,1,0:T(2,128)S(1)} %get-tuple-element.316, f32[2,2,512]{2,1,0:T(2,128)S(1)} %copy-done.72), kind=kLoop, calls=%fused_computation.4 | loop fusion | flops 33554432 | bytes 83902464 | tf_op jit(solution)/shard_map/convert_element_type | solution.py:190
  2218.7 14.5 fusion.89
  2275.0 13.1 fusion.135
  2288.1 15.2 fusion.141
  2303.3 15.0 fusion.86
  2318.3 15.2 fusion.96
  2340.9 12.0 fusion.315
  2352.9 12.1 fusion.317
  2375.7 15.4 convolution_bitcast_fusion.7
  2394.1 238.0 %reduce-scatter.15.cloned.1.call-done = f32[4096,256]{1,0:T(8,128)} async-done(((f32[4096,1024]{1,0:T(8,128)}), f32[4096,256]{1,0:T(8,128)}) %reduce-scatter.15.cloned.1.call-update) | async-done | bytes 4194320 | tf_op jit(solution)/shard_map/reduce_scatter | solution.py:28
  2636.0 41.2 %all-reduce.6 = (f32[1024]{0:T(1024)}, f32[1024]{0:T(1024)}, f32[128]{0:T(128)}, f32[128]{0:T(128)}) all-reduce(f32[1024]{0:T(1024)S(1)} %dynamic_update_slice.6, f32[1024]{0:T(1024)S(1)} %dynamic_update_slice.7, f32[128]{0:T(128)S(1)} %copy-done.118, f32[128]{0:T(128)S(1)} %get-tuple-element.240), channel_id=1, replica_groups=mesh['rows'=8,'cols'=4] {'rows','cols'}, use_global_device_ids=true, to_apply=%region_48.49 | all-reduce | flops 2304 | bytes 18432 | tf_op jit(solution)/shard_map/psum | solution.py:296
  2677.1 17.7 psum.59
  2700.8 27.6 reduce-scatter.19.cloned.1.call-done
  2728.4 55.5 %reduce-scatter.17.cloned.1.call-done = f32[128,1,1024]{2,0,1:T(8,128)} async-done(((f32[1024,1,1024]{2,0,1:T(8,128)}), f32[128,1,1024]{2,0,1:T(8,128)}) %reduce-scatter.17.cloned.1.call-update) | async-done | bytes 524304 | tf_op jit(solution)/shard_map/reduce_scatter | solution.py:61
  (445 shorter events, 433.2 us)
Async XLA Ops:
  7.2 50.1 %all-gather.24.cloned.1.call-start = ((), (), s32[]{:S(2)}) async-start(), calls=%async_computation.23 | async-start | bytes 2359296 | tf_op jit(solution)/shard_map/all_gather | solution.py:46
  7.9 183.9 %all-gather.10.cloned.1.call-start = ((), (), s32[]{:S(2)}) async-start(), calls=%async_computation.8 | async-start | bytes 10485760 | tf_op jit(solution)/shard_map/all_gather | solution.py:24
  8.7 26.2 copy-start.111
  8.7 27.1 copy-start.61
  35.0 398.9 %all-gather.12.cloned.1.call-start = ((), (), s32[]{:S(2)}) async-start(), calls=%async_computation.9 | async-start | bytes 1179648 | tf_op jit(solution)/shard_map/all_gather | solution.py:72
  35.7 689.7 %reduce-scatter.9.cloned.1.call-start = ((), (), s32[]{:S(2)}) async-start(), calls=%async_computation.10 | async-start | bytes 20971520 | tf_op jit(solution)/shard_map/reduce_scatter | solution.py:28
  42.1 179.0 %copy-start.31 = (f32[4096,64]{0,1:T(8,128)}, f32[4096,64]{0,1:T(8,128)S(1)}, u32[]{:S(2)}) copy-start(f32[4096,64]{0,1:T(8,128)S(1)} %get-tuple-element.274) | copy-start | bytes 3145732
  222.7 145.3 %copy-start.18 = (bf16[4096,2,64]{0,2,1:T(8,128)(2,1)}, bf16[4096,2,64]{0,2,1:T(8,128)(2,1)S(1)}, u32[]{:S(2)}) copy-start(bf16[4096,2,64]{0,2,1:T(8,128)(2,1)S(1)} %get-tuple-element.263) | copy-start | bytes 3145732
  222.7 145.3 %copy-start.20 = (bf16[4096,2,64]{0,2,1:T(8,128)(2,1)}, bf16[4096,2,64]{0,2,1:T(8,128)(2,1)S(1)}, u32[]{:S(2)}) copy-start(bf16[4096,2,64]{0,2,1:T(8,128)(2,1)S(1)} %get-tuple-element.264) | copy-start | bytes 3145732
  223.9 104.9 %copy-start = (bf16[4096,2,2,64]{0,3,2,1:T(8,128)(2,1)}, bf16[4096,2,2,64]{0,3,2,1:T(8,128)(2,1)S(1)}, u32[]{:S(2)}) copy-start(bf16[4096,2,2,64]{0,3,2,1:T(8,128)(2,1)S(1)} %get-tuple-element.259) | copy-start | bytes 6291460
  223.9 104.9 %copy-start.4 = (bf16[4096,2,2,64]{0,3,2,1:T(8,128)(2,1)}, bf16[4096,2,2,64]{0,3,2,1:T(8,128)(2,1)S(1)}, u32[]{:S(2)}) copy-start(bf16[4096,2,2,64]{0,3,2,1:T(8,128)(2,1)S(1)} %get-tuple-element.260) | copy-start | bytes 6291460
  446.8 278.7 %copy-start.26 = (bf16[4096,256]{1,0:T(8,128)(2,1)S(1)}, bf16[4096,256]{1,0:T(8,128)(2,1)}, u32[]{:S(2)}) copy-start(bf16[4096,256]{1,0:T(8,128)(2,1)} %param.47) | copy-start | bytes 6291460
  446.8 307.2 %all-gather.18.cloned.1.call-start = ((), (), s32[]{:S(2)}) async-start(), calls=%async_computation.13 | async-start | bytes 1769472 | tf_op jit(solution)/shard_map/all_gather | solution.py:72
  447.4 457.2 %all-gather.20.cloned.1.call-start = ((), (), s32[]{:S(2)}) async-start(), calls=%async_computation.15 | async-start | bytes 10485760 | tf_op jit(solution)/shard_map/all_gather | solution.py:24
  447.9 489.8 %all-gather.16.cloned.1.call-start = ((), (), s32[]{:S(2)}) async-start(), calls=%async_computation.12 | async-start | bytes 3538944 | tf_op jit(solution)/shard_map/all_gather | solution.py:46
  448.8 640.3 %all-gather.14.cloned.1.call-start = ((), (), s32[]{:S(2)}) async-start(), calls=%async_computation.11 | async-start | bytes 10485760 | tf_op jit(solution)/shard_map/all_gather | solution.py:24
  751.9 675.5 %reduce-scatter.13.cloned.1.call-start = ((), (), s32[]{:S(2)}) async-start(), calls=%async_computation.16 | async-start | bytes 20971520 | tf_op jit(solution)/shard_map/reduce_scatter | solution.py:28
  1148.8 562.2 %reduce-scatter.11.cloned.1.call-start = ((), (), s32[]{:S(2)}) async-start(), calls=%async_computation.14 | async-start | bytes 20971520 | tf_op jit(solution)/shard_map/reduce_scatter | solution.py:28
  1163.3 547.8 %copy-start.40 = (bf16[4096,256]{1,0:T(8,128)(2,1)S(1)}, bf16[4096,256]{1,0:T(8,128)(2,1)}, u32[]{:S(2)}) copy-start(bf16[4096,256]{1,0:T(8,128)(2,1)} %param.57) | copy-start | bytes 6291460
  1163.3 705.4 %all-gather.22.cloned.1.call-start = ((), (), s32[]{:S(2)}) async-start(), calls=%async_computation.17 | async-start | bytes 10485760 | tf_op jit(solution)/shard_map/all_gather | solution.py:24
  1450.9 267.9 %copy-start.86 = (f32[2,2,512]{2,1,0:T(2,128)S(1)}, f32[2,2,512]{2,1,0:T(2,128)}, u32[]{:S(2)}) copy-start(f32[2,2,512]{2,1,0:T(2,128)} %copy-done.85) | copy-start | bytes 24580
  1450.9 267.9 %copy-start.90 = (f32[2,2,512]{2,1,0:T(2,128)S(1)}, f32[2,2,512]{2,1,0:T(2,128)}, u32[]{:S(2)}) copy-start(f32[2,2,512]{2,1,0:T(2,128)} %copy-done.89) | copy-start | bytes 24580
  1450.9 267.9 %copy-start.84 = (f32[2,2,512]{2,1,0:T(2,128)S(1)}, f32[2,2,512]{2,1,0:T(2,128)}, u32[]{:S(2)}) copy-start(f32[2,2,512]{2,1,0:T(2,128)} %copy-done.83) | copy-start | bytes 24580
  1450.9 267.9 %copy-start.106 = (f32[2,2,512]{2,1,0:T(2,128)S(1)}, f32[2,2,512]{2,1,0:T(2,128)}, u32[]{:S(2)}) copy-start(f32[2,2,512]{2,1,0:T(2,128)} %copy-done.105) | copy-start | bytes 24580
  1450.9 268.0 %copy-start.88 = (f32[2,2,512]{2,1,0:T(2,128)S(1)}, f32[2,2,512]{2,1,0:T(2,128)}, u32[]{:S(2)}) copy-start(f32[2,2,512]{2,1,0:T(2,128)} %copy-done.87) | copy-start | bytes 24580
  1450.9 268.0 %copy-start.92 = (f32[2,2,512]{2,1,0:T(2,128)S(1)}, f32[2,2,512]{2,1,0:T(2,128)}, u32[]{:S(2)}) copy-start(f32[2,2,512]{2,1,0:T(2,128)} %copy-done.91) | copy-start | bytes 24580
  1450.9 268.6 %copy-start.94 = (f32[2,2,512]{2,1,0:T(2,128)S(1)}, f32[2,2,512]{2,1,0:T(2,128)}, u32[]{:S(2)}) copy-start(f32[2,2,512]{2,1,0:T(2,128)} %copy-done.93) | copy-start | bytes 24580
  1450.9 268.6 %copy-start.96 = (f32[2,2,512]{2,1,0:T(2,128)S(1)}, f32[2,2,512]{2,1,0:T(2,128)}, u32[]{:S(2)}) copy-start(f32[2,2,512]{2,1,0:T(2,128)} %copy-done.95) | copy-start | bytes 24580
  1450.9 268.6 %copy-start.98 = (f32[2,2,512]{2,1,0:T(2,128)S(1)}, f32[2,2,512]{2,1,0:T(2,128)}, u32[]{:S(2)}) copy-start(f32[2,2,512]{2,1,0:T(2,128)} %copy-done.97) | copy-start | bytes 24580
  1450.9 268.6 %copy-start.100 = (f32[2,2,512]{2,1,0:T(2,128)S(1)}, f32[2,2,512]{2,1,0:T(2,128)}, u32[]{:S(2)}) copy-start(f32[2,2,512]{2,1,0:T(2,128)} %copy-done.99) | copy-start | bytes 24580
  1451.0 269.2 %copy-start.102 = (f32[2,2,512]{2,1,0:T(2,128)S(1)}, f32[2,2,512]{2,1,0:T(2,128)}, u32[]{:S(2)}) copy-start(f32[2,2,512]{2,1,0:T(2,128)} %copy-done.101) | copy-start | bytes 24580
  1451.0 269.2 %copy-start.104 = (f32[2,2,512]{2,1,0:T(2,128)S(1)}, f32[2,2,512]{2,1,0:T(2,128)}, u32[]{:S(2)}) copy-start(f32[2,2,512]{2,1,0:T(2,128)} %copy-done.103) | copy-start | bytes 24580
  1451.0 269.8 %copy-start.108 = (f32[2,2,512]{2,1,0:T(2,128)S(1)}, f32[2,2,512]{2,1,0:T(2,128)}, u32[]{:S(2)}) copy-start(f32[2,2,512]{2,1,0:T(2,128)} %copy-done.107) | copy-start | bytes 24580
  1451.0 269.8 %copy-start.110 = (f32[2,2,512]{2,1,0:T(2,128)S(1)}, f32[2,2,512]{2,1,0:T(2,128)}, u32[]{:S(2)}) copy-start(f32[2,2,512]{2,1,0:T(2,128)} %copy-done.109) | copy-start | bytes 24580
  1718.6 672.6 %reduce-scatter.21.cloned.1.call-start = ((), (), s32[]{:S(2)}) async-start(), calls=%async_computation.21 | async-start | bytes 7077888 | tf_op jit(solution)/shard_map/reduce_scatter | solution.py:61
  1719.6 276.2 %copy-start.81 = (f32[2,2,512]{2,1,0:T(2,128)}, f32[2,2,512]{2,1,0:T(2,128)S(1)}, u32[]{:S(2)}) copy-start(f32[2,2,512]{2,1,0:T(2,128)S(1)} %log_add_fusion.3) | copy-start | bytes 24580
  1741.2 127.5 %copy-start.120 = (bf16[512,1024]{1,0:T(8,128)(2,1)S(1)}, bf16[512,1024]{1,0:T(8,128)(2,1)}, u32[]{:S(2)}) copy-start(bf16[512,1024]{1,0:T(8,128)(2,1)} %all-gather.12.cloned.1.call-done) | copy-start | bytes 3145732
  1741.2 890.9 %reduce-scatter.15.cloned.1.call-start = ((), (), s32[]{:S(2)}) async-start(), calls=%async_computation.18 | async-start | bytes 20971520 | tf_op jit(solution)/shard_map/reduce_scatter | solution.py:28
  1923.9 25.0 slice-start.1
  1923.9 25.0 slice-start.2
  2181.2 28.2 %copy-start.24 = (bf16[4096,2,64]{0,2,1:T(8,128)(2,1)S(1)}, bf16[4096,2,64]{0,2,1:T(8,128)(2,1)}, u32[]{:S(2)}) copy-start(bf16[4096,2,64]{0,2,1:T(8,128)(2,1)} %copy-done.20) | copy-start | bytes 3145732
  2352.9 347.9 %reduce-scatter.23.cloned.1.call-start = ((), (), s32[]{:S(2)}) async-start(), calls=%async_computation.22 | async-start | bytes 3538944 | tf_op jit(solution)/shard_map/reduce_scatter | solution.py:91
  2365.1 363.3 %reduce-scatter.19.cloned.1.call-start = ((), (), s32[]{:S(2)}) async-start(), calls=%async_computation.20 | async-start | bytes 2359296 | tf_op jit(solution)/shard_map/reduce_scatter | solution.py:91
  2375.7 408.2 %reduce-scatter.17.cloned.1.call-start = ((), (), s32[]{:S(2)}) async-start(), calls=%async_computation.19 | async-start | bytes 4718592 | tf_op jit(solution)/shard_map/reduce_scatter | solution.py:61
  2391.1 241.0 %copy-start.27 = (bf16[4096,256]{1,0:T(8,128)(2,1)S(1)}, bf16[4096,256]{1,0:T(8,128)(2,1)}, u32[]{:S(2)}) copy-start(bf16[4096,256]{1,0:T(8,128)(2,1)} %param.47) | copy-start | bytes 6291460
  2391.1 241.0 %copy-start.76 = (f32[4096]{0:T(1024)S(1)}, f32[4096]{0:T(1024)}, u32[]{:S(2)}) copy-start(f32[4096]{0:T(1024)} %copy-done.75) | copy-start | bytes 49156
  2391.1 241.0 %copy-start.112 = (f32[256]{0:T(256)S(1)}, f32[256]{0:T(256)}, u32[]{:S(2)}) copy-start(f32[256]{0:T(256)} %copy-done.111) | copy-start | bytes 3076
  2391.2 244.8 %copy-start.118 = (f32[128]{0:T(128)S(1)}, f32[128]{0:T(128)}, u32[]{:S(2)}) copy-start(f32[128]{0:T(128)} %get-tuple-element.238) | copy-start | bytes 1540
  (104 other events, 895.5 us)
Sparse Core Ops, SparseCore 0:
  9.9 30.6 all-gather.23
  42.7 149.0 all-gather.9
  193.7 21.7 all-gather.11
  446.9 278.4 reduce-scatter.8
  727.3 26.5 all-gather.17
  755.4 149.1 all-gather.19
  907.2 30.4 all-gather.15
  940.0 149.1 all-gather.13
  1149.0 278.4 reduce-scatter.12
  1429.7 281.3 reduce-scatter.10
  1718.7 149.9 all-gather.21
  1872.3 59.9 reduce-scatter.20
  2353.0 279.1 reduce-scatter.14
  2636.3 47.0 reduce-scatter.22
  2687.1 41.2 reduce-scatter.18
  2732.5 51.3 reduce-scatter.16
where the time goes:
time: 2800 us; the launch traced here: 2790 us
  waiting for transfers between devices  1710 us (61%)
  matrix products  590 us (21%)
  other arithmetic  319 us (11%)
  blocking collectives  116 us (4%)
  local copies, waits for them, and re-layouts  42.9 us (2%)
    reduce_scatter x4, waiting for transfers between devices, scatter_features(): lax.psum_scatter(partial_sum, 'cols', scatter_dimension=1, tiled=True)  1040 us
    all_gather x4, waiting for transfers between devices, gather_features(): return lax.all_gather(values, 'cols', axis=1, tiled=True)  560 us
    convert_element_type x8, other arithmetic, attend_back(): score_grad = (chances * (chance_grad - inner_sum)).astype(jnp.bfloat16)  128 us
    dot_general x8, matrix products, attend_back(): jnp.einsum('qhgd,khd->hgqk', grad_block, values[:end_at], preferred_eleme...  102 us
    psum x4, blocking collectives, feature_total(): return lax.psum(jnp.sum(values, axis=1), 'cols')  75 us
    dot_general x8, matrix products, attend_back(): jnp.einsum('hgqk,qhgd->khd', chances.astype(jnp.bfloat16), grad_block, pr...  72.5 us
    dot_general x8, matrix products, attend(): jnp.einsum('hgqk,khd->qhgd', chances, values[:end_at], preferred_element_...  68.8 us
    dot_general x8, matrix products, block_scores(): jnp.einsum('qhgd,khd->hgqk', queries[begin_at:end_at], keys[:end_at], pre...  66.8 us
  transfers between devices with their start and end apart: 16, of which 12 were waited for; matrix products, arithmetic and copies ran while one was open for 30% of the time, Pallas kernels for 0%

commit v1 on v0

v1 whole, which is shorter than its diff:
```python
from functools import partial

import jax
import jax.numpy as jnp
from jax import lax
from jax.experimental import pallas as pl
from jax.experimental.pallas import tpu as pltpu
from jax.sharding import PartitionSpec as P

HEADS = 16
KV_HEADS = 8
HEAD = 128
DOCS = 4
PER = HEADS // KV_HEADS
WIDTH = (PER + 2) * HEAD

EPS = 1e-06
THETA = 1000000.0
LOG2E = 1.4426950408889634
SCALE = HEAD ** (-0.5)
BLOCK = 512
F32 = jnp.float32
BF16 = jnp.bfloat16


def dot(a, b, ca, cb):
    return lax.dot_general(a, b, (((ca,), (cb,)), ((), ())), preferred_element_type=F32)


def forward_kernel(lo, full, qk_ref, k_ref, v_ref, start_ref, o_ref, lse_ref, vext, acc):
    i = pl.program_id(1)
    block = qk_ref.shape[0]

    @pl.when(i == 0)
    def _():
        vext[:, :HEAD] = v_ref[...]
        vext[:, HEAD:] = jnp.ones((vext.shape[0], HEAD), BF16)

    acc[...] = jnp.zeros_like(acc)

    def step(j, masked):
        at = pl.ds(pl.multiple_of(j * block, block), block)
        keys = k_ref[at, :]
        vals = vext[at, :]
        if masked:
            place = lax.broadcasted_iota(jnp.int32, (block, block), 1) + j * block
            query = lax.broadcasted_iota(jnp.int32, (block, block), 0) + i * block
            keep = (place >= start_ref[:, :1]) & (place <= query)
        for h in range(PER):
            s = dot(qk_ref[:, h * HEAD : (h + 1) * HEAD], keys, 1, 1)
            p = jnp.exp2(s * (SCALE * LOG2E))
            if masked:
                p = jnp.where(keep, p, 0.0)
            acc[h] += dot(p.astype(BF16), vals, 1, 0)

    first = jnp.minimum(full[i], i)

    @pl.loop(lo[i], first)
    def _(j):
        step(j, True)

    @pl.loop(first, i)
    def _(j):
        step(j, False)

    step(i, True)
    for h in range(PER):
        total = acc[h, :, HEAD:]
        o_ref[:, h * HEAD : (h + 1) * HEAD] = (acc[h, :, :HEAD] / total).astype(BF16)
        lse_ref[h] = jnp.transpose(jnp.log2(total))[:8]


def backward_kernel(
    last, full, q_ref, k_ref, v_ref, do_ref, o_ref, lse_ref, start_ref, out_ref, dq, inner, dk, dv
):
    j = pl.program_id(1)
    block = k_ref.shape[0]
    steps = pl.num_programs(1)

    @pl.when(j == 0)
    def _():
        dq[...] = jnp.zeros_like(dq)

        @pl.loop(0, steps)
        def _(i):
            at = pl.ds(pl.multiple_of(i * block, block), block)
            for h in range(PER):
                cols = slice(h * HEAD, (h + 1) * HEAD)
                term = do_ref[at, cols].astype(F32) * o_ref[at, cols].astype(F32)
                row = jnp.sum(term, axis=1, keepdims=True)
                inner[h, :, at] = jnp.transpose(jnp.broadcast_to(row, (block, HEAD)))[:8]

    dk[...] = jnp.zeros_like(dk)
    dv[...] = jnp.zeros_like(dv)
    keys = k_ref[...]
    vals = v_ref[...]

    def step(i, masked):
        at = pl.ds(pl.multiple_of(i * block, block), block)
        if masked:
            place = lax.broadcasted_iota(jnp.int32, (block, block), 0) + j * block
            query = lax.broadcasted_iota(jnp.int32, (block, block), 1) + i * block
            keep = (place >= start_ref[:1, at]) & (place <= query)
        for h in range(PER):
            cols = slice(h * HEAD, (h + 1) * HEAD)
            q = q_ref[at, cols]
            do = do_ref[at, cols]
            s = dot(keys, q, 1, 1)
            p = jnp.exp2(s * (SCALE * LOG2E) - lse_ref[h, :1, at])
            if masked:
                p = jnp.where(keep, p, 0.0)
            dp = dot(vals, do, 1, 1)
            ds = (p * (dp - inner[h, :1, at])).astype(BF16)
            dv[...] += dot(p.astype(BF16), do, 1, 0)
            dk[...] += dot(ds, q, 1, 0)
            dq[at, cols] += dot(ds, keys, 0, 0)

    step(j, True)
    middle = jnp.maximum(full[j], j) + 1

    @pl.loop(j + 1, middle)
    def _(i):
        step(i, False)

    @pl.loop(middle, last[j] + 1)
    def _(i):
        step(i, True)

    here = pl.ds(pl.multiple_of(j * block, block), block)
    out_ref[here, PER * HEAD : (PER + 1) * HEAD] = (dk[...] * SCALE).astype(BF16)
    out_ref[here, (PER + 1) * HEAD :] = dv[...].astype(BF16)

    @pl.when(j == steps - 1)
    def _():
        out_ref[:, : PER * HEAD] = (dq[...] * SCALE).astype(BF16)


def attend(qkv, start, block):
    length, width = qkv.shape
    groups = width // WIDTH
    steps = length // block
    blocked = start.reshape(steps, block)
    lo = blocked[:, 0] // block
    full = (blocked[:, -1] + block - 1) // block
    wide = jnp.broadcast_to(start[:, None], (length, HEAD))
    return pl.pallas_call(
        forward_kernel,
        grid_spec=pltpu.PrefetchScalarGridSpec(
            num_scalar_prefetch=2,
            grid=(groups, steps),
            in_specs=[
                pl.BlockSpec((block, PER * HEAD), lambda g, i, *_: (i, g * 2)),
                pl.BlockSpec((length, HEAD), lambda g, i, *_: (0, g * 4 + 2)),
                pl.BlockSpec((length, HEAD), lambda g, i, *_: (0, g * 4 + 3)),
                pl.BlockSpec((block, HEAD), lambda g, i, *_: (i, 0)),
            ],
            out_specs=[
                pl.BlockSpec((block, PER * HEAD), lambda g, i, *_: (i, g)),
                pl.BlockSpec((PER, 8, block), lambda g, i, *_: (g, 0, i)),
            ],
            scratch_shapes=[
                pltpu.VMEM((length, 2 * HEAD), BF16),
                pltpu.VMEM((PER, block, 2 * HEAD), F32),
            ],
        ),
        out_shape=[
            jax.ShapeDtypeStruct((length, groups * PER * HEAD), BF16),
            jax.ShapeDtypeStruct((groups * PER, 8, length), F32),
        ],
        compiler_params=pltpu.CompilerParams(vmem_limit_bytes=40 * 2**20),
        cost_estimate=pl.CostEstimate(
            flops=groups * PER * length * length * HEAD * 4,
            bytes_accessed=length * width * 4,
            transcendentals=groups * PER * length * length // 2,
        ),
        name="attend",
    )(lo, full, qkv, qkv, qkv, wide)


def attend_back(qkv, mixed, lse, grad, start, block):
    length, width = qkv.shape
    groups = width // WIDTH
    steps = length // block
    blocked = start.reshape(steps, block)
    index = jnp.arange(steps, dtype=jnp.int32)
    last = jnp.sum((blocked[:, 0] // block)[None, :] <= index[:, None], axis=1, dtype=jnp.int32) - 1
    full = jnp.sum(blocked[:, -1][None, :] <= (index * block)[:, None], axis=1, dtype=jnp.int32) - 1
    wide = jnp.broadcast_to(start[None, :], (8, length))
    return pl.pallas_call(
        backward_kernel,
        grid_spec=pltpu.PrefetchScalarGridSpec(
            num_scalar_prefetch=2,
            grid=(groups, steps),
            in_specs=[
                pl.BlockSpec((length, PER * HEAD), lambda g, j, *_: (0, g * 2)),
                pl.BlockSpec((block, HEAD), lambda g, j, *_: (j, g * 4 + 2)),
                pl.BlockSpec((block, HEAD), lambda g, j, *_: (j, g * 4 + 3)),
                pl.BlockSpec((length, PER * HEAD), lambda g, j, *_: (0, g)),
                pl.BlockSpec((length, PER * HEAD), lambda g, j, *_: (0, g)),
                pl.BlockSpec((PER, 8, length), lambda g, j, *_: (g, 0, 0)),
                pl.BlockSpec((8, length), lambda g, j, *_: (0, 0)),
            ],
            out_specs=pl.BlockSpec((length, WIDTH), lambda g, j, *_: (0, g)),
            scratch_shapes=[
                pltpu.VMEM((length, PER * HEAD), F32),
                pltpu.VMEM((PER, 8, length), F32),
                pltpu.VMEM((block, HEAD), F32),
                pltpu.VMEM((block, HEAD), F32),
            ],
        ),
        out_shape=jax.ShapeDtypeStruct((length, width), BF16),
        compiler_params=pltpu.CompilerParams(vmem_limit_bytes=48 * 2**20),
        cost_estimate=pl.CostEstimate(
            flops=groups * PER * length * length * HEAD * 10,
            bytes_accessed=length * width * 8,
            transcendentals=groups * PER * length * length // 2,
        ),
        name="attend_back",
    )(last, full, qkv, qkv, qkv, grad, mixed, lse, wide)


def rotate(values, cosine, sine_table):
    half_size = values.shape[-1] // 2
    front = values[..., :half_size]
    back_half = values[..., half_size:]
    return jnp.concatenate(
        [front * cosine - back_half * sine_table, back_half * cosine + front * sine_table], axis=-1
    )


def head_norm(values, scaling):
    return values * lax.rsqrt(jnp.mean(values * values, axis=-1, keepdims=True) + EPS) * scaling


def heads_local(query_raw, key_raw, query_gain, key_gain, cosine, sine_table):
    queries = rotate(
        head_norm(query_raw, query_gain), cosine[:, None, None], sine_table[:, None, None]
    )
    keys = rotate(head_norm(key_raw, key_gain), cosine[:, None], sine_table[:, None])
    return (queries, keys)


def norm_scale(values):
    return lax.rsqrt(jnp.mean(values * values, axis=1, keepdims=True) + EPS)


def norm_backward(values, scale, scaling, gradient):
    inner_sum = jnp.mean(gradient * scaling * values, axis=1, keepdims=True)
    back_grad = scale * scaling * gradient - values * scale * scale * scale * inner_sum
    gain_part = jnp.sum(gradient * values * scale, axis=0)
    return (back_grad, gain_part)


def local(
    tokens,
    qkv_weight,
    out_weight,
    expand_weight,
    down_weight,
    attn_gain,
    mlp_gain,
    query_gain,
    key_gain,
    segment_ids,
    cotangent,
):
    rows = lax.axis_size("rows")
    cols = lax.axis_size("cols")
    length, local_width = tokens.shape
    width = local_width * cols
    paired = cols == 4 and rows % 2 == 0
    share = 2 if paired else cols // 2
    count = length // cols
    if paired:
        team_axis = "rows"
        team_sets = [[2 * i, 2 * i + 1] for i in range(rows // 2)]
        seat = lax.axis_index("rows") % 2
    else:
        team_axis = "cols"
        team_sets = [[share * i + k for k in range(share)] for i in range(2)]
        seat = lax.axis_index("cols") % share

    def team(values, split, concat):
        return lax.all_to_all(values, team_axis, split, concat, axis_index_groups=team_sets)

    def spread(values):
        if paired:
            values = team(values.reshape(2, 2, count, local_width), 1, 0)
        values = values.reshape(cols, count, local_width)
        return lax.all_to_all(values, "cols", 0, 1).reshape(count, width)

    def collect(values):
        values = lax.all_to_all(values.reshape(count, cols, local_width), "cols", 1, 0)
        if paired:
            values = team(values.reshape(2, 2, count, local_width), 0, 1)
        return values.reshape(length, local_width)

    def to_heads(values):
        part = values.shape[1] // share
        return team(values.reshape(count, share, part), 1, 0).reshape(share * count, part)

    def to_tokens(values):
        part = values.shape[1]
        return team(values.reshape(share, count, part), 0, 1).reshape(count, share * part)

    def gather_in(weight):
        weight = lax.all_gather(weight, "cols", axis=weight.ndim - 1, tiled=True)
        return lax.all_gather(weight, "rows", axis=0, tiled=True)

    def gather_out(weight):
        weight = lax.all_gather(weight, "cols", axis=0, tiled=True)
        return lax.all_gather(weight, "rows", axis=1, tiled=True)

    def scatter_in(grad):
        grad = grad.astype(BF16)
        grad = lax.psum_scatter(grad, "rows", scatter_dimension=0, tiled=True)
        grad = lax.psum_scatter(grad, "cols", scatter_dimension=grad.ndim - 1, tiled=True)
        return grad.astype(F32)

    def scatter_out(grad):
        grad = grad.astype(BF16)
        grad = lax.psum_scatter(grad, "rows", scatter_dimension=1, tiled=True)
        grad = lax.psum_scatter(grad, "cols", scatter_dimension=0, tiled=True)
        return grad.astype(F32)

    segment = segment_ids[0]
    member = segment[:, None] == jnp.arange(DOCS, dtype=jnp.int32)[None, :]
    sizes = jnp.sum(member.astype(jnp.int32), axis=0, dtype=jnp.int32)
    starts = jnp.cumsum(sizes, dtype=jnp.int32) - sizes
    doc_start = jnp.sum(jnp.where(member, starts[None, :], 0), axis=1, dtype=jnp.int32)
    position = jnp.arange(length, dtype=jnp.int32) - doc_start
    turn = jnp.sum(jnp.where(sizes == length // 2, starts, 0), dtype=jnp.int32)
    position = jnp.roll(position, -turn)
    if paired:
        both = lax.all_gather(position, "rows", axis_index_groups=team_sets)
        halves = both.reshape(cols, length // 2)
        which = lax.axis_index("cols")
    else:
        halves = position.reshape(2, length // 2)
        which = lax.axis_index("cols") // share
    half = lax.dynamic_index_in_dim(halves, which, 0, keepdims=False)
    start = jnp.arange(length // 2, dtype=jnp.int32) - half
    own = lax.dynamic_slice_in_dim(half, seat * count, count).astype(F32)
    frequency = THETA ** (-jnp.arange(0, HEAD, 2, dtype=F32) / HEAD)
    angles = own[:, None] * frequency[None, :]
    cosine, sine_table = jnp.cos(angles), jnp.sin(angles)
    block = min(BLOCK, length // 2)

    x = spread(jnp.roll(tokens, -turn, axis=0)).astype(F32)
    w_qkv = gather_in(qkv_weight)
    w_out = gather_out(out_weight)
    w_expand = gather_in(expand_weight)
    w_down = gather_out(down_weight)
    grad_low = spread(jnp.roll(cotangent, -turn, axis=0))

    scale_one = norm_scale(x)
    normed_one = (x * scale_one * attn_gain).astype(BF16)
    grouped = dot(normed_one, w_qkv, 1, 0).reshape(count, KV_HEADS, PER + 2, HEAD)
    query_raw = grouped[:, :, :PER]
    key_raw = grouped[:, :, PER]
    local_heads = partial(heads_local, cosine=cosine, sine_table=sine_table)
    (queries, keys), pullback = jax.vjp(local_heads, query_raw, key_raw, query_gain, key_gain)
    packed = jnp.concatenate(
        [queries.astype(BF16), keys.astype(BF16)[:, :, None], grouped[:, :, PER + 1 :].astype(BF16)],
        axis=2,
    )
    qkv = to_heads(packed.reshape(count, KV_HEADS * WIDTH))
    mixed_heads, lse = attend(qkv, start, block)
    mixed = to_tokens(mixed_heads)

    hidden = x + dot(mixed, w_out, 1, 0)
    scale_two = norm_scale(hidden)
    normed_two = (hidden * scale_two * mlp_gain).astype(BF16)
    gate_up = jnp.einsum("tk,ksf->tsf", normed_two, w_expand, preferred_element_type=F32)
    gate = gate_up[:, 0]
    upper = gate_up[:, 1]
    sigmoid_gate = jax.nn.sigmoid(gate)
    silu_gate = gate * sigmoid_gate
    activation = (silu_gate * upper).astype(BF16)
    output = collect((hidden + dot(activation, w_down, 1, 0)).astype(BF16))
    output = jnp.roll(output, turn, axis=0)

    act_grad = dot(grad_low, w_down, 1, 1)
    down_grad = scatter_out(dot(activation, grad_low, 0, 0))
    gate_grad = act_grad * upper * sigmoid_gate * (1.0 + gate * (1.0 - sigmoid_gate))
    upper_grad = act_grad * silu_gate
    expand_back = jnp.stack([gate_grad, upper_grad], axis=1).astype(BF16)
    normed_grad_two = jnp.einsum("tsf,ksf->tk", expand_back, w_expand, preferred_element_type=F32)
    expand_grad = scatter_in(
        jnp.einsum("tk,tsf->ksf", normed_two, expand_back, preferred_element_type=F32)
    )
    back_two, gain_two_grad = norm_backward(hidden, scale_two, mlp_gain, normed_grad_two)
    hidden_grad = grad_low.astype(F32) + back_two
    hidden_low = hidden_grad.astype(BF16)
    mixed_grad = to_heads(dot(hidden_low, w_out, 1, 1).astype(BF16))
    out_grad = scatter_out(dot(mixed, hidden_low, 0, 0))

    back = to_tokens(attend_back(qkv, mixed_heads, lse, mixed_grad, start, block))
    back = back.reshape(count, KV_HEADS, PER + 2, HEAD)
    query_raw_grad, key_raw_grad, query_gain_part, key_gain_part = pullback(
        (back[:, :, :PER].astype(F32), back[:, :, PER].astype(F32))
    )
    qkv_back = jnp.concatenate(
        [
            query_raw_grad.astype(BF16),
            key_raw_grad.astype(BF16)[:, :, None],
            back[:, :, PER + 1 :],
        ],
        axis=2,
    ).reshape(count, KV_HEADS * WIDTH)
    normed_grad_one = dot(qkv_back, w_qkv, 1, 1)
    qkv_grad = scatter_in(dot(normed_one, qkv_back, 0, 0))
    back_one, gain_one_grad = norm_backward(x, scale_one, attn_gain, normed_grad_one)
    input_grad = collect((hidden_grad + back_one).astype(BF16))
    input_grad = jnp.roll(input_grad, turn, axis=0).astype(F32)
    gains = lax.psum(
        jnp.concatenate([gain_one_grad, gain_two_grad, query_gain_part, key_gain_part]),
        ("rows", "cols"),
    )
    return (
        output,
        input_grad,
        qkv_grad,
        out_grad,
        expand_grad,
        down_grad,
        gains[:width],
        gains[width : 2 * width],
        gains[2 * width : 2 * width + HEAD],
        gains[2 * width + HEAD :],
    )


def solution(mesh):
    return jax.shard_map(
        local,
        mesh=mesh,
        in_specs=(
            P("rows", "cols"),
            P("rows", "cols"),
            P("cols", "rows"),
            P("rows", None, "cols"),
            P("cols", "rows"),
            P(),
            P(),
            P(),
            P(),
            P("rows", None),
            P("rows", "cols"),
        ),
        out_specs=(
            P("rows", "cols"),
            P("rows", "cols"),
            P("rows", "cols"),
            P("cols", "rows"),
            P("rows", None, "cols"),
            P("cols", "rows"),
            P(),
            P(),
            P(),
            P(),
        ),
        check_vma=False,
    )
```

time: 2800 us -> 987 us (0.35)
  waiting for transfers between devices: 1710 us -> 179 us
  matrix products: 590 us -> 192 us
  other arithmetic: 319 us -> 98 us
  Pallas kernels: 0 us -> 116 us
  blocking collectives: 116 us -> 207 us
  local copies, waits for them, and re-layouts: 42.9 us -> 125 us
  starting transfers between devices: 0.83 us -> 47.3 us
    reduce_scatter x8 -> x6, waiting for transfers between devices: 1120 us -> 112 us  [the longest x2 80.7 us: scatter_in(): grad = lax.psum_scatter(grad, 'rows', scatter_dimension=0, tiled=True)]
    all_gather x8 -> x6, waiting for transfers between devices: 583 us -> 52.5 us  [the longest x2 52.5 us: gather_in(): weight = lax.all_gather(weight, 'cols', axis=weight.ndim - 1, tiled=True)]
    dot_general x60 -> x12, matrix products: 590 us -> 192 us  [the longest x9 125 us: dot(): lax.dot_general(a, b, (((ca,), (cb,)), ((), ())), preferred_element_type=...]
    convert_element_type x13 -> x9, other arithmetic: 146 us -> 26.1 us  [the longest x1 7.18 us: local(): input_grad = jnp.roll(input_grad, turn, axis=0).astype(F32)]
    pallas_call x0 -> x2, Pallas kernels: none -> 116 us  [the longest x1 77.4 us: attend_back(): pl.pallas_call(backward_kernel, grid_spec=pltpu.PrefetchScalarGridSpec(nu...]
    all_to_all x0 -> x4, blocking collectives: none -> 85.5 us  [the longest x1 52.2 us: spread(): return lax.all_to_all(values, 'cols', 0, 1).reshape(count, width)]
    all_gather x0 -> x3, blocking collectives: none -> 81.7 us  [the longest x2 79.7 us: gather_out(): weight = lax.all_gather(weight, 'cols', axis=0, tiled=True)]
    psum x5 -> x1, blocking collectives: 116 us -> 39.9 us  [local(): lax.psum(jnp.concatenate([gain_one_grad, gain_two_grad, query_gain_part,...]
  transfers between devices with their start and end apart: 16 -> 22, of which waited for: 12 -> 7; matrix products, arithmetic and copies ran while one was open for 30% -> 34% of each run, Pallas kernels for 0% -> 12%
where the time goes in v1:
time: 987 us; the launch traced here: 982 us
  blocking collectives  207 us (21%)
  matrix products  192 us (19%)
  waiting for transfers between devices  179 us (18%)
  local copies, waits for them, and re-layouts  125 us (13%)
  Pallas kernels  116 us (12%)
  other arithmetic  98 us (10%)
  starting transfers between devices  47.3 us (5%)
  between operations  17.6 us (2%)
    dot_general x9, matrix products, dot(): lax.dot_general(a, b, (((ca,), (cb,)), ((), ())), preferred_element_type=...  125 us
    reduce_scatter x2, waiting for transfers between devices, scatter_in(): grad = lax.psum_scatter(grad, 'rows', scatter_dimension=0, tiled=True)  80.7 us
    all_gather x2, blocking collectives, gather_out(): weight = lax.all_gather(weight, 'cols', axis=0, tiled=True)  79.7 us
    pallas_call x1, Pallas kernels, attend_back(): pl.pallas_call(backward_kernel, grid_spec=pltpu.PrefetchScalarGridSpec(nu...  77.4 us
    all_gather x2, waiting for transfers between devices, gather_in(): weight = lax.all_gather(weight, 'cols', axis=weight.ndim - 1, tiled=True)  52.5 us
    all_to_all x1, blocking collectives, spread(): return lax.all_to_all(values, 'cols', 0, 1).reshape(count, width)  52.2 us
    another operation x8, local copies, waits for them, and re-layouts, team(): lax.all_to_all(values, team_axis, split, concat, axis_index_groups=team_s...  43.2 us
    unnamed x112, local copies, waits for them, and re-layouts  42.3 us
  transfers between devices with their start and end apart: 22, of which 7 were waited for; matrix products, arithmetic and copies ran while one was open for 34% of the time, Pallas kernels for 12%

profile of v1, /device:TPU:0, one launch (start us, length us, event | category | flops | bytes accessed | tf_op | source)
XLA Modules:
  0.0 982.2 jit_solution(5214452305387794874)
XLA Ops:
  9.8 30.4 %all-gather.8.cloned.1.call-done = bf16[128,4096]{1,0:T(8,128)(2,1)} async-done(((bf16[128,1024]{1,0:T(8,128)(2,1)}), bf16[128,4096]{1,0:T(8,128)(2,1)}) %all-gather.8.cloned.1.call-update) | async-done | bytes 1048592 | tf_op jit(solution)/shard_map/all_gather | solution.py:307
  40.3 18.1 %all_gather.34 = bf16[2048,128]{1,0:T(8,128)(2,1)} all-gather(bf16[512,128]{1,0:T(8,128)(2,1)} %param.15), channel_id=1, replica_groups=mesh['rows'=8,'cols'=4] {'cols'}, dimensions={0}, use_global_device_ids=true | all-gather | bytes 655360 | tf_op jit(solution)/shard_map/all_gather | solution.py:311
  58.5 22.1 %all-gather.14.cloned.1.call-done = bf16[128,2,3072]{2,0,1:T(8,128)(2,1)} async-done(((bf16[128,2,768]{2,0,1:T(8,128)(2,1)}), bf16[128,2,3072]{2,0,1:T(8,128)(2,1)}) %all-gather.14.cloned.1.call-update) | async-done | bytes 1572880 | tf_op jit(solution)/shard_map/all_gather | solution.py:307
  82.9 10.1 %fusion.43 = (bf16[4096,256]{1,0:T(8,128)(2,1)}, bf16[4096,256]{1,0:T(8,128)(2,1)S(1)}) fusion(s32[]{:T(128)S(6)} %select_n.72, bf16[4096,256]{1,0:T(8,128)(2,1)S(1)} %copy-done.22, bf16[4096,256]{1,0:T(8,128)(2,1)} %param.13), kind=kLoop, calls=%fused_computation.92 | loop fusion | flops 8388608 | bytes 8388612 | tf_op jit(solution)/shard_map/jit(_roll_dynamic)/concatenate | solution.py:354
  101.3 8.6 all_to_all.174
  109.8 52.2 %all_to_all.175 = bf16[4,1024,1,256]{3,1,2,0:T(8,128)(2,1)} all-to-all(bf16[4,1024,1,256]{3,1,2,0:T(8,128)(2,1)S(1)} %bitcast.266), channel_id=1, replica_groups=mesh['rows'=8,'cols'=4] {'cols'}, dimensions={0} | all-to-all | bytes 4194304 | tf_op jit(solution)/shard_map/all_to_all | solution.py:290
  166.5 61.6 %all_gather.38 = bf16[3072,128]{1,0:T(8,128)(2,1)} all-gather(bf16[768,128]{1,0:T(8,128)(2,1)S(1)} %copy-done.30), channel_id=1, replica_groups=mesh['rows'=8,'cols'=4] {'cols'}, dimensions={0}, use_global_device_ids=true | all-gather | bytes 983040 | tf_op jit(solution)/shard_map/all_gather | solution.py:311
  243.8 12.0 %copy.184 = bf16[4096,1024]{1,0:T(8,128)(2,1)} copy(bf16[4096,1024]{0,1:T(8,128)(2,1)} %bitcast.260) | data formatting | bytes 16777216 | tf_op jit(solution)/shard_map/dot_general | solution.py:27
  255.8 16.9 %fusion.69 = f32[1024,8,4,128]{0,3,2,1:T(8,128)} fusion(bf16[1024,1024,1,1]{0,1,3,2:T(8,128)(2,1)} %bitcast.272, bf16[8,4,128,1024]{3,2,1,0:T(8,128)(2,1)} %bitcast.264), kind=kOutput, calls=%fused_computation.161 | convolution fusion | flops 8589934592 | bytes 27262976 | tf_op jit(solution)/shard_map/dot_general | solution.py:27
  275.4 6.0 multiply_reduce_fusion.2
  288.2 4.6 multiply_multiply_fusion
  292.8 5.4 subtract_convert_fusion
  299.0 11.9 %all_to_all.176 = bf16[1,1024,2,2048]{1,3,0,2:T(8,128)(2,1)} all-to-all(bf16[1,1024,2,2048]{1,3,0,2:T(8,128)(2,1)S(1)} %bitcast.254), channel_id=1, replica_groups={{0,4},{8,12},{16,20},{24,28},{1,5},{9,13},{17,21},{25,29},{2,6},{10,14}..., dimensions={2} | all-to-all | bytes 16777216 | tf_op jit(solution)/shard_map/all_to_all | solution.py:284
  310.9 11.7 %copy.190 = bf16[2,1,1024,1,2048]{4,2,0,3,1:T(8,128)(2,1)} copy(bf16[2,1,1024,1,2048]{2,4,0,3,1:T(8,128)(2,1)} %bitcast.255) | data formatting | bytes 16777216 | tf_op jit(solution)/shard_map/all_to_all | solution.py:284
  326.3 38.4 %attend.1 = (bf16[2048,1024]{1,0:T(8,128)(2,1)S(1)}, f32[8,8,2048]{2,1,0:T(8,128)S(1)}) custom-call(s32[4]{0:T(128)S(1)} %and_select_fusion.1.lo, s32[4]{0:T(128)S(1)} %and_select_fusion.full, bf16[2048,2048]{1,0:T(8,128)(2,1)S(1)} %bitcast.246, bf16[2048,2048]{1,0:T(8,128)(2,1)S(1)} %bitcast.247, bf16[2048,2048]{1,0:T(8,128)(2,1)S(1)} %bitcast.248, ...), custom_call_target="tpu_custom_call" | custom-call | flops 17179869184 | bytes 16777216 | tf_op jit(solution)/shard_map/attend/pallas_call | solution.py:146
  366.7 6.2 copy.191
  372.9 5.6 all-to-all-start.3
  378.5 10.1 %reduce-scatter.25.cloned.1.call-start = ((), (), s32[]{:S(2)}) async-start(), calls=%async_computation.32 | async-start | bytes 4718592
  388.7 10.3 %multiply_reduce_fusion.5 = (f32[1024]{0:T(1024)S(1)}, f32[1024,1024]{0,1:T(8,128)}) fusion(bf16[1024,2048]{0,1:T(8,128)(2,1)} %bitcast.31, bf16[2048,1024]{1,0:T(8,128)(2,1)} %all-gather.12.cloned.1.call-done, bf16[4,1024,1,256]{1,3,0,2:T(8,128)(2,1)S(1)} %copy.183), kind=kOutput, calls=%fused_computation.82 | convolution fusion | flops 4299160576 | bytes 14684160 | tf_op jit(solution)/shard_map/dot_general | solution.py:27
  399.0 22.5 %fusion.58 = f32[1024,2,3072]{2,0,1:T(8,128)} fusion(bf16[1024,2,3072]{2,0,1:T(8,128)(2,1)} %all-gather.16.cloned.1.call-done, f32[1024,1024]{0,1:T(8,128)} %get-tuple-element.138, f32[1024]{0:T(1024)S(1)} %copy-done.44, f32[1024]{0:T(1024)S(1)} %add_rsqrt_fusion), kind=kOutput, calls=%fused_computation.117 | convolution fusion | flops 12888047616 | bytes 41951232 | tf_op jit(solution)/shard_map/tk,ksf->tsf/dot_general | solution.py:374
  421.5 19.2 %fusion.17 = (bf16[1024,1,3072]{2,0,1:T(8,128)(2,1)}, bf16[1024,1,3072]{2,0,1:T(8,128)(2,1)}) fusion(f32[1024,2,3072]{2,0,1:T(8,128)} %fusion.58, bf16[1024,1024]{0,1:T(8,128)(2,1)S(1)} %bitcast.270, bf16[3072,1024]{1,0:T(8,128)(2,1)} %all-gather.18.cloned.1.call-done), kind=kOutput, calls=%fused_computation.34 | convolution fusion | flops 6483345408 | bytes 46137344 | tf_op jit(solution)/shard_map/dot_general | solution.py:27
  440.7 23.9 %fusion.39 = (f32[1024]{0:T(1024)}, f32[1024]{0:T(1024)S(1)}, f32[1024,1024,1]{0,1,2:T(8,128)S(1)}) fusion(f32[1024,1024]{0,1:T(8,128)} %get-tuple-element.138, f32[1024]{0:T(1024)S(1)} %add_rsqrt_fusion, f32[1024]{0:T(1024)S(1)} %copy-done.44, bf16[1024,2,3072]{2,0,1:T(8,128)(2,1)} %all-gather.16.cloned.1.call-done, ...), kind=kOutput, calls=%fused_computation.74 | convolution fusion | flops 12897482752 | bytes 33570816 | tf_op jit(solution)/shard_map/tsf,ksf->tk/dot_general | solution.py:388
  468.0 8.4 convolution_convert_fusion.1
  476.4 6.5 copy.214
  483.8 10.4 %convolution_convert_fusion.2 = bf16[1024,2048]{1,0:T(8,128)(2,1)} fusion(bf16[2048,1024]{1,0:T(8,128)(2,1)} %all-gather.12.cloned.1.call-done, f32[1024,1024]{0,1:T(8,128)} %copy-done.9), kind=kOutput, calls=%fused_computation.88 | convolution fusion | flops 4298113024 | bytes 12582912 | tf_op jit(solution)/shard_map/dot_general | solution.py:27
  494.2 8.0 broadcast_in_dim_reshape.25
  502.1 6.2 copy.200
  508.3 5.6 all-to-all-start.8
  514.0 14.3 %fusion.18 = bf16[3072,1024]{1,0:T(8,128)(2,1)} fusion(bf16[1024,1024]{0,1:T(8,128)(2,1)S(1)} %bitcast.271, f32[1024,2,3072]{2,0,1:T(8,128)} %fusion.58), kind=kOutput, calls=%fused_computation.35 | convolution fusion | flops 6464471040 | bytes 33554432 | tf_op jit(solution)/shard_map/dot_general | solution.py:27
  528.3 8.7 copy.216
  537.7 77.4 %attend_back.1 = bf16[2048,2048]{1,0:T(8,128)(2,1)} custom-call(s32[4]{0:T(128)S(1)} %broadcast_add_fusion.1.last, s32[4]{0:T(128)S(1)} %broadcast_add_fusion.full, bf16[2048,2048]{1,0:T(8,128)(2,1)} %bitcast.243, bf16[2048,2048]{1,0:T(8,128)(2,1)} %bitcast.244, bf16[2048,2048]{1,0:T(8,128)(2,1)} %bitcast.245, bf16[2048,1024]{1,0:T(8,128)(2,1)} %bitcast.56.do_ref, ...), custom_call_target="tpu_custom_call" | custom-call | flops 42949672960 | bytes 33554432 | tf_op jit(solution)/shard_map/attend_back/pallas_call | solution.py:189
  615.2 11.8 %copy.201 = bf16[2,1024,1,2048]{1,3,2,0:T(8,128)(2,1)} copy(bf16[2,1024,1,2048]{3,1,0,2:T(8,128)(2,1)} %bitcast.263) | data formatting | bytes 16777216 | tf_op jit(solution)/shard_map/broadcast_in_dim;reshape | solution.py:284
  627.0 12.9 %all_to_all.177 = bf16[2,1024,1,2048]{1,3,2,0:T(8,128)(2,1)S(1)} all-to-all(bf16[2,1024,1,2048]{1,3,2,0:T(8,128)(2,1)} %copy.201), channel_id=1, replica_groups={{0,4},{8,12},{16,20},{24,28},{1,5},{9,13},{17,21},{25,29},{2,6},{10,14}..., dimensions={0} | all-to-all | bytes 16777216 | tf_op jit(solution)/shard_map/all_to_all | solution.py:284
  647.4 7.2 multiply_add_fusion.1
  654.7 5.4 multiply_reduce_fusion
  670.5 4.8 fusion.8
  682.5 11.3 %convolution_convert_fusion = bf16[1024,4096]{1,0:T(8,128)(2,1)} fusion(bf16[1024,1024]{0,1:T(8,128)(2,1)S(1)} %bitcast.273, bf16[1024,4096]{0,1:T(8,128)(2,1)S(1)} %bitcast.261), kind=kOutput, calls=%fused_computation.28 | convolution fusion | flops 8594128896 | bytes 18874368 | tf_op jit(solution)/shard_map/dot_general | solution.py:27
  694.5 20.9 %fusion.11 = bf16[1024,2,3072]{2,0,1:T(8,128)(2,1)} fusion(bf16[1024,1,3072]{2,0,1:T(8,128)(2,1)} %get-tuple-element.118, bf16[1024,1,3072]{2,0,1:T(8,128)(2,1)} %get-tuple-element.117, f32[1024,1024]{0,1:T(8,128)} %get-tuple-element.138, f32[1024]{0:T(1024)S(1)} %copy-done.45, f32[1024]{0:T(1024)S(1)} %copy-done.38), kind=kOutput, calls=%fused_computation.26 | convolution fusion | flops 12919504896 | bytes 29368320 | tf_op jit(solution)/shard_map/tk,tsf->ksf/dot_general | solution.py:390
  720.1 19.5 %add_convert_fusion = bf16[1024,1024]{0,1:T(8,128)(2,1)} fusion(f32[1024,1024]{0,1:T(8,128)} %get-tuple-element.138, bf16[3072,1024]{1,0:T(8,128)(2,1)} %all-gather.18.cloned.1.call-done, f32[1024,2,3072]{2,0,1:T(8,128)} %fusion.58), kind=kOutput, calls=%fused_computation.80 | convolution fusion | flops 6463422464 | bytes 37748736 | tf_op jit(solution)/shard_map/dot_general | solution.py:27
  744.2 18.6 %reduce-scatter.13.cloned.1.call-done = bf16[128,4096]{1,0:T(8,128)(2,1)} async-done(((bf16[1024,4096]{1,0:T(8,128)(2,1)}), bf16[128,4096]{1,0:T(8,128)(2,1)}) %reduce-scatter.13.cloned.1.call-update) | async-done | bytes 1048592 | tf_op jit(solution)/shard_map/reduce_scatter | solution.py:316
  762.8 14.6 %fusion.33 = (f32[1024]{0:T(1024)S(1)}, f32[1024]{0:T(1024)S(1)}, f32[1024,1024]{0,1:T(8,128)S(1)}) fusion(bf16[4,1024,1,256]{1,3,0,2:T(8,128)(2,1)S(1)} %copy-done.7, f32[1024]{0:T(1024)S(1)} %copy-done.33, f32[1024]{0:T(1024)S(1)} %copy-done.36, bf16[1024,4096]{1,0:T(8,128)(2,1)} %all-gather.10.cloned.1.call-done, bf16[1024,4096]{0,1:T(8,128)(2,1)} %bitcast.262), kind=kOutput, calls=%fused_computation.65 | convolution fusion | flops 8597272576 | bytes 23085056 | tf_op jit(solution)/shard_map/dot_general | solution.py:27
  780.1 12.9 %all-to-all-done.4 = bf16[1,1024,4,256]{1,3,0,2:T(8,128)(2,1)} async-done(((bf16[1,1024,4,256]{1,3,0,2:T(8,128)(2,1)}), bf16[1,1024,4,256]{1,3,0,2:T(8,128)(2,1)}, u32[]{:S(2)}, u32[]{:S(2)}) %all-to-all-start.4) | async-done | bytes 2097184 | tf_op jit(solution)/shard_map/all_to_all | solution.py:293
  796.8 62.1 %reduce-scatter.19.cloned.1.call-done = bf16[128,2,3072]{2,0,1:T(8,128)(2,1)} async-done(((bf16[1024,2,3072]{2,0,1:T(8,128)(2,1)}), bf16[128,2,3072]{2,0,1:T(8,128)(2,1)}) %reduce-scatter.19.cloned.1.call-update) | async-done | bytes 1572880 | tf_op jit(solution)/shard_map/reduce_scatter | solution.py:316
  860.3 39.9 %psum.7 = f32[2304]{0:T(1024)S(1)} all-reduce(f32[2304]{0:T(1024)S(1)} %pad_maximum_fusion.7), channel_id=1, replica_groups=mesh['rows'=8,'cols'=4] {'rows','cols'}, use_global_device_ids=true, to_apply=%region_26.28 | all-reduce | flops 2304 | bytes 18432 | tf_op jit(solution)/shard_map/psum | solution.py:416
  905.3 4.9 all-to-all-start.5
  921.9 7.6 fusion.44
  929.4 7.2 fusion.42
  941.7 31.4 %reduce-scatter.21.cloned.1.call-done = bf16[128,2,768]{2,0,1:T(8,128)(2,1)} async-done(((bf16[128,2,3072]{2,0,1:T(8,128)(2,1)}), bf16[128,2,768]{2,0,1:T(8,128)(2,1)}) %reduce-scatter.21.cloned.1.call-update) | async-done | bytes 393232 | tf_op jit(solution)/shard_map/reduce_scatter | solution.py:317
  (226 shorter events, 118.6 us)
Async XLA Ops:
  7.2 73.4 %copy-start.31 = (s32[1,4096]{1,0:T(1,128)S(1)}, s32[1,4096]{1,0:T(1,128)}, u32[]{:S(2)}) copy-start(s32[1,4096]{1,0:T(1,128)} %param.22) | copy-start | bytes 49156
  7.2 75.7 %copy-start.22 = (bf16[4096,256]{1,0:T(8,128)(2,1)S(1)}, bf16[4096,256]{1,0:T(8,128)(2,1)}, u32[]{:S(2)}) copy-start(bf16[4096,256]{1,0:T(8,128)(2,1)} %param.23) | copy-start | bytes 6291460
  7.2 33.1 %all-gather.8.cloned.1.call-start = ((), (), s32[]{:S(2)}) async-start(), calls=%async_computation.20 | async-start | bytes 1310720 | tf_op jit(solution)/shard_map/all_gather | solution.py:307
  7.9 72.6 %all-gather.14.cloned.1.call-start = ((), (), s32[]{:S(2)}) async-start(), calls=%async_computation.23 | async-start | bytes 1966080 | tf_op jit(solution)/shard_map/all_gather | solution.py:307
  9.8 234.0 %all-gather.10.cloned.1.call-start = ((), (), s32[]{:S(2)}) async-start(), calls=%async_computation.21 | async-start | bytes 9437184 | tf_op jit(solution)/shard_map/all_gather | solution.py:308
  40.3 348.4 %all-gather.12.cloned.1.call-start = ((), (), s32[]{:S(2)}) async-start(), calls=%async_computation.22 | async-start | bytes 4718592 | tf_op jit(solution)/shard_map/all_gather | solution.py:312
  58.4 340.5 %all-gather.16.cloned.1.call-start = ((), (), s32[]{:S(2)}) async-start(), calls=%async_computation.24 | async-start | bytes 14155776 | tf_op jit(solution)/shard_map/all_gather | solution.py:308
  94.4 6.8 all-to-all-start
  109.8 56.7 %copy-start.30 = (bf16[768,128]{1,0:T(8,128)(2,1)S(1)}, bf16[768,128]{1,0:T(8,128)(2,1)}, u32[]{:S(2)}) copy-start(bf16[768,128]{1,0:T(8,128)(2,1)} %param.17) | copy-start | bytes 589828
  109.8 122.4 %copy-start.35 = (f32[1024]{0:T(1024)S(1)}, f32[1024]{0:T(1024)}, u32[]{:S(2)}) copy-start(f32[1024]{0:T(1024)} %param.18) | copy-start | bytes 12292
  162.0 75.8 %all-to-all-start.7 = ((bf16[4,1024,1,256]{3,1,2,0:T(8,128)(2,1)}), bf16[4,1024,1,256]{3,1,2,0:T(8,128)(2,1)}, u32[]{:S(2)}, u32[]{:S(2)}) async-start(bf16[4,1024,1,256]{3,1,2,0:T(8,128)(2,1)} %bitcast.47), calls=%async_computation.7 | async-start | bytes 4194304 | tf_op jit(solution)/shard_map/all_to_all | solution.py:290
  166.4 255.1 %all-gather.18.cloned.1.call-start = ((), (), s32[]{:S(2)}) async-start(), calls=%async_computation.25 | async-start | bytes 7077888 | tf_op jit(solution)/shard_map/all_gather | solution.py:312
  234.0 58.8 %copy-start.16 = (f32[1024,64]{0,1:T(8,128)}, f32[1024,64]{0,1:T(8,128)S(1)}, u32[]{:S(2)}) copy-start(f32[1024,64]{0,1:T(8,128)S(1)} %get-tuple-element.133) | copy-start | bytes 786436
  234.0 58.8 %copy-start.18 = (f32[1024,64]{0,1:T(8,128)}, f32[1024,64]{0,1:T(8,128)S(1)}, u32[]{:S(2)}) copy-start(f32[1024,64]{0,1:T(8,128)S(1)} %get-tuple-element.134) | copy-start | bytes 786436
  237.2 151.4 %copy-start.6 = (bf16[4,1024,1,256]{1,3,0,2:T(8,128)(2,1)}, bf16[4,1024,1,256]{1,3,0,2:T(8,128)(2,1)S(1)}, u32[]{:S(2)}) copy-start(bf16[4,1024,1,256]{1,3,0,2:T(8,128)(2,1)S(1)} %copy.183) | copy-start | bytes 6291460
  237.7 6.1 copy-start.32
  272.7 12.3 %copy-start.2 = (f32[1024,8,4,128]{0,3,2,1:T(8,128)S(1)}, f32[1024,8,4,128]{0,3,2,1:T(8,128)}, u32[]{:S(2)}) copy-start(f32[1024,8,4,128]{0,3,2,1:T(8,128)} %fusion.69) | copy-start | bytes 50331652
  372.9 15.7 %all-to-all-start.3 = ((bf16[2,1024,1,1024]{1,3,2,0:T(8,128)(2,1)}), bf16[2,1024,1,1024]{1,3,2,0:T(8,128)(2,1)}, u32[]{:S(2)}, u32[]{:S(2)}) async-start(bf16[2,1024,1,1024]{1,3,2,0:T(8,128)(2,1)} %copy.191), calls=%async_computation.3 | async-start | bytes 8388608 | tf_op jit(solution)/shard_map/all_to_all | solution.py:284
  378.5 337.0 %reduce-scatter.25.cloned.1.call-start = ((), (), s32[]{:S(2)}) async-start(), calls=%async_computation.32 | async-start | bytes 4718592
  388.7 10.3 %copy-start.44 = (f32[1024]{0:T(1024)S(1)}, f32[1024]{0:T(1024)}, u32[]{:S(2)}) copy-start(f32[1024]{0:T(1024)} %param.19) | copy-start | bytes 12292
  399.0 65.6 %copy-start.37 = (f32[1024]{0:T(1024)}, f32[1024]{0:T(1024)S(1)}, u32[]{:S(2)}) copy-start(f32[1024]{0:T(1024)S(1)} %add_rsqrt_fusion) | copy-start | bytes 12292
  399.0 22.5 %copy-start.14 = (bf16[1,1024,4,1,256]{1,4,2,3,0:T(8,128)(2,1)S(1)}, bf16[1,1024,4,1,256]{1,4,2,3,0:T(8,128)(2,1)}, u32[]{:S(2)}) copy-start(bf16[1,1024,4,1,256]{1,4,2,3,0:T(8,128)(2,1)} %copy.199) | copy-start | bytes 6291460
  440.7 23.9 %copy-start.20 = (f32[1024,1024]{0,1:T(8,128)S(1)}, f32[1024,1024]{0,1:T(8,128)}, u32[]{:S(2)}) copy-start(f32[1024,1024]{0,1:T(8,128)} %get-tuple-element.138) | copy-start | bytes 12582916
  508.3 28.8 %all-to-all-start.8 = ((bf16[1,1024,2,1024]{3,1,0,2:T(8,128)(2,1)}), bf16[1,1024,2,1024]{3,1,0,2:T(8,128)(2,1)}, u32[]{:S(2)}, u32[]{:S(2)}) async-start(bf16[1,1024,2,1024]{3,1,0,2:T(8,128)(2,1)} %copy.200), calls=%async_computation.8 | async-start | bytes 8388608 | tf_op jit(solution)/shard_map/all_to_all | solution.py:284
  513.9 203.8 %reduce-scatter.27.cloned.1.call-start = ((), (), s32[]{:S(2)}) async-start(), calls=%async_computation.33 | async-start | bytes 7077888
  537.0 225.7 %reduce-scatter.13.cloned.1.call-start = ((), (), s32[]{:S(2)}) async-start(), calls=%async_computation.26 | async-start | bytes 9437184 | tf_op jit(solution)/shard_map/reduce_scatter | solution.py:316
  627.0 27.7 %slice-start = ((s8[16777216]{0:T(1024)(128)(4,1)}), s8[4194304]{0:T(1024)(128)(4,1)S(1)}, s32[]{:S(2)}) async-start(s8[16777216]{0:T(1024)(128)(4,1)} %bitcast.250), calls=%async_computation.34 | async-start | bytes 8388608
  627.0 27.7 %slice-start.1 = ((s8[16777216]{0:T(1024)(128)(4,1)}), s8[4194304]{0:T(1024)(128)(4,1)S(1)}, s32[]{:S(2)}) async-start(s8[16777216]{0:T(1024)(128)(4,1)} %bitcast.250), calls=%async_computation.35 | async-start | bytes 8388608
  643.1 11.6 %slice-start.2 = ((s8[16777216]{0:T(1024)(128)(4,1)}), s8[4194304]{0:T(1024)(128)(4,1)S(1)}, s32[]{:S(2)}) async-start(s8[16777216]{0:T(1024)(128)(4,1)} %bitcast.250), calls=%async_computation.36 | async-start | bytes 8388608
  647.4 7.2 slice-start.3
  647.4 7.3 copy-start.40
  654.7 6.2 copy-start.5
  675.3 7.3 copy-start.21
  693.8 165.1 %reduce-scatter.19.cloned.1.call-start = ((), (), s32[]{:S(2)}) async-start(), calls=%async_computation.29 | async-start | bytes 14155776 | tf_op jit(solution)/shard_map/reduce_scatter | solution.py:316
  715.5 221.1 %reduce-scatter.17.cloned.1.call-start = ((), (), s32[]{:S(2)}) async-start(), calls=%async_computation.28 | async-start | bytes 655360 | tf_op jit(solution)/shard_map/reduce_scatter | solution.py:323
  717.7 220.6 %reduce-scatter.23.cloned.1.call-start = ((), (), s32[]{:S(2)}) async-start(), calls=%async_computation.31 | async-start | bytes 983040 | tf_op jit(solution)/shard_map/reduce_scatter | solution.py:323
  739.5 23.3 %copy-start.7 = (bf16[4,1024,1,256]{1,3,0,2:T(8,128)(2,1)S(1)}, bf16[4,1024,1,256]{1,3,0,2:T(8,128)(2,1)}, u32[]{:S(2)}) copy-start(bf16[4,1024,1,256]{1,3,0,2:T(8,128)(2,1)} %copy-done.6) | copy-start | bytes 6291460
  739.5 23.3 %copy-start.33 = (f32[1024]{0:T(1024)S(1)}, f32[1024]{0:T(1024)}, u32[]{:S(2)}) copy-start(f32[1024]{0:T(1024)} %copy-done.32) | copy-start | bytes 12292
  739.5 23.3 %copy-start.36 = (f32[1024]{0:T(1024)S(1)}, f32[1024]{0:T(1024)}, u32[]{:S(2)}) copy-start(f32[1024]{0:T(1024)} %param.18) | copy-start | bytes 12292
  739.5 53.4 %all-to-all-start.4 = ((bf16[1,1024,4,256]{1,3,0,2:T(8,128)(2,1)}), bf16[1,1024,4,256]{1,3,0,2:T(8,128)(2,1)}, u32[]{:S(2)}, u32[]{:S(2)}) async-start(bf16[1,1024,4,256]{1,3,0,2:T(8,128)(2,1)} %bitcast.274), calls=%async_computation.4 | async-start | bytes 4194304 | tf_op jit(solution)/shard_map/all_to_all | solution.py:293
  744.1 195.8 %reduce-scatter.15.cloned.1.call-start = ((), (), s32[]{:S(2)}) async-start(), calls=%async_computation.27 | async-start | bytes 1310720 | tf_op jit(solution)/shard_map/reduce_scatter | solution.py:317
  762.8 14.6 %copy-start.10 = (f32[1024,1024]{0,1:T(8,128)S(1)}, f32[1024,1024]{0,1:T(8,128)}, u32[]{:S(2)}) copy-start(f32[1024,1024]{0,1:T(8,128)} %copy-done.9) | copy-start | bytes 12582916
  780.1 80.2 %copy-start.43 = (f32[1024]{0:T(1024)S(1)}, f32[1024]{0:T(1024)}, u32[]{:S(2)}) copy-start(f32[1024]{0:T(1024)} %get-tuple-element.109) | copy-start | bytes 12292
  780.1 80.2 %copy-start.46 = (f32[128]{0:T(128)S(1)}, f32[128]{0:T(128)}, u32[]{:S(2)}) copy-start(f32[128]{0:T(128)} %get-tuple-element.107) | copy-start | bytes 1540
  793.0 112.3 %all-to-all-start.10 = ((bf16[1,1024,4,256]{1,3,0,2:T(8,128)(2,1)}), bf16[1,1024,4,256]{1,3,0,2:T(8,128)(2,1)S(1)}, u32[]{:S(2)}, u32[]{:S(2)}) async-start(bf16[1,1024,4,256]{1,3,0,2:T(8,128)(2,1)} %bitcast.258), calls=%async_computation.10 | async-start | bytes 4194304 | tf_op jit(solution)/shard_map/all_to_all | solution.py:293
  796.8 176.4 %reduce-scatter.21.cloned.1.call-start = ((), (), s32[]{:S(2)}) async-start(), calls=%async_computation.30 | async-start | bytes 1966080 | tf_op jit(solution)/shard_map/reduce_scatter | solution.py:317
  905.3 7.9 all-to-all-start.5
  913.1 7.2 all-to-all-start.11
  (27 other events, 62.9 us)
Sparse Core Ops, SparseCore 0:
  9.6 30.6 all-gather.7
  42.4 38.1 all-gather.13
  82.5 53.7 all-gather.9
  138.0 37.4 all-gather.11
  177.2 72.1 all-gather.15
  251.1 46.6 all-gather.17
  483.1 49.5 reduce-scatter.24
  537.2 61.0 reduce-scatter.26
  694.0 68.7 reduce-scatter.12
  766.5 92.3 reduce-scatter.18
  861.9 21.7 reduce-scatter.16
  886.6 21.5 reduce-scatter.22
  910.6 26.3 reduce-scatter.14
  939.2 33.9 reduce-scatter.20

commit v2 on v1

--- a/solution.py
+++ b/solution.py
@@ -308,18 +308,20 @@
         return lax.all_gather(weight, "rows", axis=0, tiled=True)
 
     def gather_out(weight):
-        weight = lax.all_gather(weight, "cols", axis=0, tiled=True)
-        return lax.all_gather(weight, "rows", axis=1, tiled=True)
-
-    def scatter_in(grad):
-        grad = grad.astype(BF16)
-        grad = lax.psum_scatter(grad, "rows", scatter_dimension=0, tiled=True)
+        weight = lax.all_gather(weight, "rows", axis=1, tiled=True)
+        return lax.all_gather(weight, "cols", axis=0, tiled=True)
+
+    def rows_in(grad):
+        return lax.psum_scatter(grad, "rows", scatter_dimension=0, tiled=True)
+
+    def cols_in(grad):
         grad = lax.psum_scatter(grad, "cols", scatter_dimension=grad.ndim - 1, tiled=True)
         return grad.astype(F32)
 
-    def scatter_out(grad):
-        grad = grad.astype(BF16)
-        grad = lax.psum_scatter(grad, "rows", scatter_dimension=1, tiled=True)
+    def rows_out(grad):
+        return lax.psum_scatter(grad, "rows", scatter_dimension=1, tiled=True)
+
+    def cols_out(grad):
         grad = lax.psum_scatter(grad, "cols", scatter_dimension=0, tiled=True)
         return grad.astype(F32)
 
@@ -346,8 +348,12 @@
     cosine, sine_table = jnp.cos(angles), jnp.sin(angles)
     block = min(BLOCK, length // 2)
 
-    x = spread(jnp.roll(tokens, -turn, axis=0)).astype(F32)
     w_qkv = gather_in(qkv_weight)
+    x_low = spread(jnp.roll(tokens, -turn, axis=0))
+    x_low, out_weight, expand_weight, down_weight = lax.optimization_barrier(
+        (x_low, out_weight, expand_weight, down_weight)
+    )
+    x = x_low.astype(F32)
     w_out = gather_out(out_weight)
     w_expand = gather_in(expand_weight)
     w_down = gather_out(down_weight)
@@ -377,25 +383,44 @@
     sigmoid_gate = jax.nn.sigmoid(gate)
     silu_gate = gate * sigmoid_gate
     activation = (silu_gate * upper).astype(BF16)
-    output = collect((hidden + dot(activation, w_down, 1, 0)).astype(BF16))
-    output = jnp.roll(output, turn, axis=0)
+    result = (hidden + dot(activation, w_down, 1, 0)).astype(BF16)
 
     act_grad = dot(grad_low, w_down, 1, 1)
-    down_grad = scatter_out(dot(activation, grad_low, 0, 0))
+    down_part = dot(activation, grad_low, 0, 0).astype(BF16)
     gate_grad = act_grad * upper * sigmoid_gate * (1.0 + gate * (1.0 - sigmoid_gate))
     upper_grad = act_grad * silu_gate
     expand_back = jnp.stack([gate_grad, upper_grad], axis=1).astype(BF16)
     normed_grad_two = jnp.einsum("tsf,ksf->tk", expand_back, w_expand, preferred_element_type=F32)
-    expand_grad = scatter_in(
-        jnp.einsum("tk,tsf->ksf", normed_two, expand_back, preferred_element_type=F32)
-    )
+    expand_part = jnp.einsum(
+        "tk,tsf->ksf", normed_two, expand_back, preferred_element_type=F32
+    ).astype(BF16)
+    normed_grad_two, down_part, expand_part = lax.optimization_barrier(
+        (normed_grad_two, down_part, expand_part)
+    )
+    expand_part = rows_in(expand_part)
+    down_part = rows_out(down_part)
     back_two, gain_two_grad = norm_backward(hidden, scale_two, mlp_gain, normed_grad_two)
     hidden_grad = grad_low.astype(F32) + back_two
     hidden_low = hidden_grad.astype(BF16)
-    mixed_grad = to_heads(dot(hidden_low, w_out, 1, 1).astype(BF16))
-    out_grad = scatter_out(dot(mixed, hidden_low, 0, 0))
-
-    back = to_tokens(attend_back(qkv, mixed_heads, lse, mixed_grad, start, block))
+    mixed_grad, out_part, result = lax.optimization_barrier(
+        (
+            dot(hidden_low, w_out, 1, 1).astype(BF16),
+            dot(mixed, hidden_low, 0, 0).astype(BF16),
+            result,
+        )
+    )
+    output = collect(result)
+    mixed_grad = to_heads(mixed_grad)
+    out_grad = cols_out(rows_out(out_part))
+
+    back = attend_back(qkv, mixed_heads, lse, mixed_grad, start, block)
+    back, output, expand_part, down_part = lax.optimization_barrier(
+        (back, output, expand_part, down_part)
+    )
+    expand_grad = cols_in(expand_part)
+    down_grad = cols_out(down_part)
+    output = jnp.roll(output, turn, axis=0)
+    back = to_tokens(back)
     back = back.reshape(count, KV_HEADS, PER + 2, HEAD)
     query_raw_grad, key_raw_grad, query_gain_part, key_gain_part = pullback(
         (back[:, :, :PER].astype(F32), back[:, :, PER].astype(F32))
@@ -409,7 +434,7 @@
         axis=2,
     ).reshape(count, KV_HEADS * WIDTH)
     normed_grad_one = dot(qkv_back, w_qkv, 1, 1)
-    qkv_grad = scatter_in(dot(normed_one, qkv_back, 0, 0))
+    qkv_grad = cols_in(rows_in(dot(normed_one, qkv_back, 0, 0).astype(BF16)))
     back_one, gain_one_grad = norm_backward(x, scale_one, attn_gain, normed_grad_one)
     input_grad = collect((hidden_grad + back_one).astype(BF16))
     input_grad = jnp.roll(input_grad, turn, axis=0).astype(F32)

time: 987 us -> 1030 us (1.044)
  waiting for transfers between devices: 179 us -> 307 us
  blocking collectives: 207 us -> 88 us
  local copies, waits for them, and re-layouts: 125 us -> 187 us
  starting transfers between devices: 47.3 us -> 34.9 us
  other arithmetic: 98 us -> 87.4 us
    all_to_all x1 -> x2, waiting for transfers between devices: 0.01 us -> 107 us  [spread(): return lax.all_to_all(values, 'cols', 0, 1).reshape(count, width)]
    all_gather x2 -> x0, blocking collectives: 79.7 us -> none  [gather_out(): weight = lax.all_gather(weight, 'cols', axis=0, tiled=True)]
    all_to_all x1 -> x0, blocking collectives: 52.2 us -> none  [spread(): return lax.all_to_all(values, 'cols', 0, 1).reshape(count, width)]
    all_gather x2 -> x4, waiting for transfers between devices: 0.02 us -> 45.2 us  [the longest x2 24.6 us: gather_out(): return lax.all_gather(weight, 'cols', axis=0, tiled=True)]
    unnamed x112 -> x107, local copies, waits for them, and re-layouts: 42.3 us -> 70.1 us
    reduce_scatter x6, waiting for transfers between devices: 112 us -> 90.3 us  [the longest x2 46.3 us: rows_in(): return lax.psum_scatter(grad, 'rows', scatter_dimension=0, tiled=True)]
    reshape x0 -> x1, local copies, waits for them, and re-layouts: none -> 20.5 us  [local(): dot(normed_one, w_qkv, 1, 0).reshape(count, KV_HEADS, PER + 2, HEAD)]
    all_gather x2, waiting for transfers between devices: 0.01 us -> 16.8 us  [gather_in(): return lax.all_gather(weight, 'rows', axis=0, tiled=True)]
  transfers between devices with their start and end apart: 22 -> 23, of which waited for: 7 -> 11; matrix products, arithmetic and copies ran while one was open for 34% -> 36% of each run, Pallas kernels for 12% -> 11%
where the time goes in v2:
time: 1030 us
  waiting for transfers between devices  307 us (30%)
  local copies, waits for them, and re-layouts  187 us (18%)
  matrix products  187 us (18%)
  Pallas kernels  117 us (11%)
  blocking collectives  88 us (9%)
  other arithmetic  87.4 us (8%)
  starting transfers between devices  34.9 us (3%)
  between operations  17.6 us (2%)
    dot_general x9, matrix products, dot(): lax.dot_general(a, b, (((ca,), (cb,)), ((), ())), preferred_element_type=...  124 us
    all_to_all x2, waiting for transfers between devices, spread(): return lax.all_to_all(values, 'cols', 0, 1).reshape(count, width)  107 us
    pallas_call x1, Pallas kernels, attend_back(): pl.pallas_call(backward_kernel, grid_spec=pltpu.PrefetchScalarGridSpec(nu...  78.4 us
    unnamed x107, local copies, waits for them, and re-layouts  70.1 us
    reduce_scatter x2, waiting for transfers between devices, rows_in(): return lax.psum_scatter(grad, 'rows', scatter_dimension=0, tiled=True)  46.3 us
    all_to_all x5, blocking collectives, team(): lax.all_to_all(values, team_axis, split, concat, axis_index_groups=team_s...  46 us
    another operation x8, local copies, waits for them, and re-layouts, team(): lax.all_to_all(values, team_axis, split, concat, axis_index_groups=team_s...  40.1 us
    psum x1, blocking collectives, local(): lax.psum(jnp.concatenate([gain_one_grad, gain_two_grad, query_gain_part,...  39.9 us
  transfers between devices with their start and end apart: 23, of which 11 were waited for; matrix products, arithmetic and copies ran while one was open for 36% of the time, Pallas kernels for 11%

profile of v2, /device:TPU:0, one launch (start us, length us, event | category | flops | bytes accessed | tf_op | source)
XLA Modules:
  0.0 1025.5 jit_solution(15454680729789102700)
XLA Ops:
  10.2 5.8 fusion.42
  16.1 6.3 all_to_all.180
  22.4 6.5 all-to-all-start.1
  29.6 64.6 %all-to-all-done.1 = bf16[4,1024,1,256]{3,1,2,0:T(8,128)(2,1)S(1)} async-done(((bf16[4,1024,1,256]{3,1,2,0:T(8,128)(2,1)}), bf16[4,1024,1,256]{3,1,2,0:T(8,128)(2,1)S(1)}, u32[]{:S(2)}, u32[]{:S(2)}) %all-to-all-start.1) | async-done | bytes 2097184 | tf_op jit(solution)/shard_map/all_to_all | solution.py:290
  100.8 20.6 %all-gather.14.cloned.1.call-done = bf16[512,1024]{1,0:T(8,128)(2,1)} async-done(((bf16[512,128]{1,0:T(8,128)(2,1)}), bf16[512,1024]{1,0:T(8,128)(2,1)}) %all-gather.14.cloned.1.call-update) | async-done | bytes 1048592 | tf_op jit(solution)/shard_map/all_gather | solution.py:311
  121.5 39.2 %all-gather.22.cloned.1.call-done = bf16[128,2,3072]{2,0,1:T(8,128)(2,1)} async-done(((bf16[128,2,768]{2,0,1:T(8,128)(2,1)}), bf16[128,2,3072]{2,0,1:T(8,128)(2,1)}) %all-gather.22.cloned.1.call-update) | async-done | bytes 1572880 | tf_op jit(solution)/shard_map/all_gather | solution.py:307
  162.4 6.3 all_to_all.181
  179.3 42.8 %all-to-all-done.4 = bf16[4,1024,1,256]{3,1,2,0:T(8,128)(2,1)} async-done(((bf16[4,1024,1,256]{3,1,2,0:T(8,128)(2,1)}), bf16[4,1024,1,256]{3,1,2,0:T(8,128)(2,1)}, u32[]{:S(2)}, u32[]{:S(2)}) %all-to-all-start.4) | async-done | bytes 2097184 | tf_op jit(solution)/shard_map/all_to_all | solution.py:290
  226.5 16.8 %all-gather.12.cloned.1.call-done = bf16[1024,4096]{1,0:T(8,128)(2,1)} async-done(((bf16[128,4096]{1,0:T(8,128)(2,1)}), bf16[1024,4096]{1,0:T(8,128)(2,1)}) %all-gather.12.cloned.1.call-update) | async-done | bytes 8388624 | tf_op jit(solution)/shard_map/all_gather | solution.py:308
  243.4 15.0 %fusion.53 = f32[1024,4096]{1,0:T(8,128)} fusion(bf16[1024,4096]{1,0:T(8,128)(2,1)} %all-gather.12.cloned.1.call-done, bf16[1024,1024]{0,1:T(8,128)(2,1)S(1)} %bitcast.211, f32[1024]{0:T(1024)S(1)} %copy-done.41, f32[1024]{0:T(1024)S(1)} %add_rsqrt_fusion.1), kind=kOutput, calls=%fused_computation.102 | convolution fusion | flops 8594128896 | bytes 27271168 | tf_op jit(solution)/shard_map/dot_general | solution.py:27
  258.4 20.5 %reshape.322 = f32[1024,8,4,128]{3,2,1,0:T(4,128)} reshape(f32[1024,4096]{1,0:T(8,128)} %fusion.53) | data formatting | bytes 33554432 | tf_op jit(solution)/shard_map/reshape | solution.py:364
  278.9 9.4 slice.80
  288.3 10.0 slice.83
  303.1 10.9 %copy.236 = f32[1024,8,1,128]{0,3,1,2:T(8,128)} copy(f32[1024,8,1,128]{3,2,1,0:T(1,128)} %slice.80) | data formatting | bytes 8388608
  317.4 10.5 %copy.239 = bf16[1024,8,1,128]{0,3,2,1:T(8,128)(2,1)} copy(bf16[1024,8,1,128]{3,2,1,0:T(2,128)(2,1)} %slice.83) | data formatting | bytes 4194304
  327.9 14.0 %copy.238 = f32[1024,8,2,128]{0,3,2,1:T(8,128)} copy(f32[1024,8,2,128]{3,2,1,0:T(2,128)} %slice.77) | data formatting | bytes 16777216
  357.6 13.6 %all_to_all.182 = bf16[1,1024,2,2048]{1,3,0,2:T(8,128)(2,1)} all-to-all(bf16[1,1024,2,2048]{1,3,0,2:T(8,128)(2,1)S(1)} %bitcast.207), channel_id=1, replica_groups={{0,4},{8,12},{16,20},{24,28},{1,5},{9,13},{17,21},{25,29},{2,6},{10,14}..., dimensions={2} | all-to-all | bytes 16777216 | tf_op jit(solution)/shard_map/all_to_all | solution.py:284
  371.2 11.8 %copy.205 = bf16[2,1,1024,1,2048]{4,2,0,3,1:T(8,128)(2,1)} copy(bf16[2,1,1024,1,2048]{2,4,0,3,1:T(8,128)(2,1)} %bitcast.208) | data formatting | bytes 16777216 | tf_op jit(solution)/shard_map/all_to_all | solution.py:284
  386.8 38.4 %attend.1 = (bf16[2048,1024]{1,0:T(8,128)(2,1)S(1)}, f32[8,8,2048]{2,1,0:T(8,128)S(1)}) custom-call(s32[4]{0:T(128)S(1)} %and_select_fusion.1.lo, s32[4]{0:T(128)S(1)} %and_select_fusion.full, bf16[2048,2048]{1,0:T(8,128)(2,1)S(1)} %bitcast.197, bf16[2048,2048]{1,0:T(8,128)(2,1)S(1)} %bitcast.198, bf16[2048,2048]{1,0:T(8,128)(2,1)S(1)} %bitcast.199, ...), custom_call_target="tpu_custom_call" | custom-call | flops 17179869184 | bytes 16777216 | tf_op jit(solution)/shard_map/attend/pallas_call | solution.py:146
  427.2 6.2 copy.209
  443.5 10.3 %multiply_reduce_fusion.6 = (f32[1024]{0:T(1024)S(1)}, f32[1024,1024]{0,1:T(8,128)}) fusion(bf16[1024,2048]{0,1:T(8,128)(2,1)} %bitcast.33, bf16[2048,1024]{1,0:T(8,128)(2,1)} %all-gather.16.cloned.1.call-done, bf16[1024,1024]{0,1:T(8,128)(2,1)S(1)} %bitcast.212), kind=kOutput, calls=%fused_computation.78 | convolution fusion | flops 4299160576 | bytes 14684160 | tf_op jit(solution)/shard_map/dot_general | solution.py:27
  453.8 22.6 %fusion.59 = f32[1024,2,3072]{2,0,1:T(8,128)} fusion(bf16[1024,2,3072]{2,0,1:T(8,128)(2,1)} %all-gather.24.cloned.1.call-done, f32[1024,1024]{0,1:T(8,128)} %get-tuple-element.156, f32[1024]{0:T(1024)S(1)} %copy-done.36, f32[1024]{0:T(1024)S(1)} %add_rsqrt_fusion), kind=kOutput, calls=%fused_computation.113 | convolution fusion | flops 12888047616 | bytes 41951232 | tf_op jit(solution)/shard_map/tk,ksf->tsf/dot_general | solution.py:380
  476.4 14.1 %fusion.18 = bf16[3072,1024]{1,0:T(8,128)(2,1)} fusion(bf16[1024,1024]{0,1:T(8,128)(2,1)S(1)} %bitcast.229, f32[1024,2,3072]{2,0,1:T(8,128)} %fusion.59), kind=kOutput, calls=%fused_computation.40 | convolution fusion | flops 6464471040 | bytes 33554432 | tf_op jit(solution)/shard_map/dot_general | solution.py:27
  490.6 24.6 %all-gather.20.cloned.1.call-done = bf16[3072,1024]{1,0:T(8,128)(2,1)} async-done(((bf16[768,1024]{1,0:T(8,128)(2,1)}), bf16[3072,1024]{1,0:T(8,128)(2,1)}) %all-gather.20.cloned.1.call-update) | async-done | bytes 6291472 | tf_op jit(solution)/shard_map/all_gather | solution.py:312
  515.1 19.3 %fusion.17 = (bf16[1024,1,3072]{2,0,1:T(8,128)(2,1)}, bf16[1024,1,3072]{2,0,1:T(8,128)(2,1)}) fusion(f32[1024,2,3072]{2,0,1:T(8,128)} %fusion.59, bf16[1024,1024]{0,1:T(8,128)(2,1)S(1)} %bitcast.230, bf16[3072,1024]{1,0:T(8,128)(2,1)} %all-gather.20.cloned.1.call-done), kind=kOutput, calls=%fused_computation.39 | convolution fusion | flops 6483345408 | bytes 46137344 | tf_op jit(solution)/shard_map/dot_general | solution.py:27
  534.4 20.2 %fusion.11 = bf16[1024,2,3072]{2,0,1:T(8,128)(2,1)} fusion(bf16[1024,1,3072]{2,0,1:T(8,128)(2,1)} %get-tuple-element.136, bf16[1024,1,3072]{2,0,1:T(8,128)(2,1)} %get-tuple-element.135, f32[1024,1024]{0,1:T(8,128)} %get-tuple-element.156, f32[1024]{0:T(1024)S(1)} %copy-done.36, f32[1024]{0:T(1024)S(1)} %add_rsqrt_fusion), kind=kOutput, calls=%fused_computation.31 | convolution fusion | flops 12919504896 | bytes 29368320 | tf_op jit(solution)/shard_map/tk,tsf->ksf/dot_general | solution.py:394
  554.6 20.7 %fusion.37 = f32[1024,1024]{1,0:T(8,128)} fusion(bf16[1024,2,3072]{2,0,1:T(8,128)(2,1)} %all-gather.24.cloned.1.call-done, bf16[1024,1,3072]{2,0,1:T(8,128)(2,1)} %get-tuple-element.136, bf16[1024,1,3072]{2,0,1:T(8,128)(2,1)} %get-tuple-element.135), kind=kOutput, calls=%fused_computation.84 | convolution fusion | flops 12891193344 | bytes 29360128 | tf_op jit(solution)/shard_map/tsf,ksf->tk/dot_general | solution.py:393
  575.3 8.7 copy.232
  584.9 5.8 copy.212
  590.7 6.5 multiply_reduce_fusion.4
  599.9 9.9 convolution_convert_fusion.1
  609.8 6.2 convolution_convert_fusion.2
  616.0 18.9 %add_convert_fusion = bf16[1024,1024]{0,1:T(8,128)(2,1)} fusion(f32[1024,1024]{0,1:T(8,128)} %get-tuple-element.156, bf16[3072,1024]{1,0:T(8,128)(2,1)} %all-gather.20.cloned.1.call-done, f32[1024,2,3072]{2,0,1:T(8,128)} %fusion.59), kind=kOutput, calls=%fused_computation.74 | convolution fusion | flops 6463422464 | bytes 37748736 | tf_op jit(solution)/shard_map/dot_general | solution.py:27
  634.9 8.0 broadcast_in_dim_reshape.24
  654.1 6.7 copy.234
  664.7 78.4 %attend_back.1 = bf16[2048,2048]{1,0:T(8,128)(2,1)} custom-call(s32[4]{0:T(128)S(1)} %broadcast_add_fusion.1.last, s32[4]{0:T(128)S(1)} %broadcast_add_fusion.full, bf16[2048,2048]{1,0:T(8,128)(2,1)} %bitcast.194, bf16[2048,2048]{1,0:T(8,128)(2,1)} %bitcast.195, bf16[2048,2048]{1,0:T(8,128)(2,1)} %bitcast.196, bf16[2048,1024]{1,0:T(8,128)(2,1)} %bitcast.46.do_ref, ...), custom_call_target="tpu_custom_call" | custom-call | flops 42949672960 | bytes 33554432 | tf_op jit(solution)/shard_map/attend_back/pallas_call | solution.py:189
  745.6 7.5 all_to_all.183
  756.9 12.0 %copy.219 = bf16[2,1024,1,2048]{1,3,2,0:T(8,128)(2,1)} copy(bf16[2,1024,1,2048]{3,1,0,2:T(8,128)(2,1)} %bitcast.221) | data formatting | bytes 16777216 | tf_op jit(solution)/shard_map/broadcast_in_dim;reshape | solution.py:284
  769.0 12.3 %all_to_all.184 = bf16[2,1024,1,2048]{1,3,2,0:T(8,128)(2,1)S(1)} all-to-all(bf16[2,1024,1,2048]{1,3,2,0:T(8,128)(2,1)} %copy.219), channel_id=1, replica_groups={{0,4},{8,12},{16,20},{24,28},{1,5},{9,13},{17,21},{25,29},{2,6},{10,14}..., dimensions={0} | all-to-all | bytes 16777216 | tf_op jit(solution)/shard_map/all_to_all | solution.py:284
  809.3 5.8 pad_maximum_fusion.2
  815.1 15.0 %convolution_convert_fusion = bf16[1024,4096]{1,0:T(8,128)(2,1)} fusion(bf16[1024,4096]{0,1:T(8,128)(2,1)} %bitcast.219, bf16[1024,1024]{0,1:T(8,128)(2,1)S(1)} %bitcast.213, f32[1024]{0:T(1024)S(1)} %copy-done.42, f32[1024]{0:T(1024)S(1)} %copy-done.34), kind=kOutput, calls=%fused_computation.33 | convolution fusion | flops 8598323200 | bytes 18882560 | tf_op jit(solution)/shard_map/dot_general | solution.py:27
  833.4 15.2 %fusion.33 = (f32[1024]{0:T(1024)S(1)}, f32[1024]{0:T(1024)S(1)}, f32[1024,1024]{0,1:T(8,128)S(1)}) fusion(bf16[1024,1024]{0,1:T(8,128)(2,1)S(1)} %bitcast.214, f32[1024]{0:T(1024)S(1)} %copy-done.34, f32[1024]{0:T(1024)S(1)} %copy-done.42, bf16[1024,4096]{1,0:T(8,128)(2,1)} %all-gather.12.cloned.1.call-done, bf16[1024,4096]{0,1:T(8,128)(2,1)} %bitcast.220), kind=kOutput, calls=%fused_computation.53 | convolution fusion | flops 8597272576 | bytes 23085056 | tf_op jit(solution)/shard_map/dot_general | solution.py:27
  856.0 46.3 %reduce-scatter.15.cloned.1.call-done = bf16[128,4096]{1,0:T(8,128)(2,1)} async-done(((bf16[1024,4096]{1,0:T(8,128)(2,1)}), bf16[128,4096]{1,0:T(8,128)(2,1)}) %reduce-scatter.15.cloned.1.call-update) | async-done | bytes 1048592 | tf_op jit(solution)/shard_map/reduce_scatter | solution.py:315
  903.6 23.3 %reduce-scatter.19.cloned.1.call-done = bf16[512,128]{1,0:T(8,128)(2,1)} async-done(((bf16[2048,128]{1,0:T(8,128)(2,1)}), bf16[512,128]{1,0:T(8,128)(2,1)}) %reduce-scatter.19.cloned.1.call-update) | async-done | bytes 131088 | tf_op jit(solution)/shard_map/reduce_scatter | solution.py:325
  928.5 39.9 %psum.7 = f32[2304]{0:T(1024)S(1)} all-reduce(f32[2304]{0:T(1024)S(1)} %pad_maximum_fusion.9), channel_id=1, replica_groups=mesh['rows'=8,'cols'=4] {'rows','cols'}, use_global_device_ids=true, to_apply=%region_26.28 | all-reduce | flops 2304 | bytes 18432 | tf_op jit(solution)/shard_map/psum | solution.py:441
  969.5 7.6 fusion.41
  991.0 7.2 fusion.40
  998.2 18.8 %reduce-scatter.17.cloned.1.call-done = bf16[128,1024]{1,0:T(8,128)(2,1)} async-done(((bf16[128,4096]{1,0:T(8,128)(2,1)}), bf16[128,1024]{1,0:T(8,128)(2,1)}) %reduce-scatter.17.cloned.1.call-update) | async-done | bytes 262160 | tf_op jit(solution)/shard_map/reduce_scatter | solution.py:318
  (228 shorter events, 146.9 us)
Async XLA Ops:
  22.4 76.2 %copy-start.28 = (bf16[128,2,768]{2,1,0:T(2,128)(2,1)S(1)}, bf16[128,2,768]{2,1,0:T(2,128)(2,1)}, u32[]{:S(2)}) copy-start(bf16[128,2,768]{2,1,0:T(2,128)(2,1)} %param.16) | copy-start | bytes 1179652
  22.4 71.8 %all-to-all-start.1 = ((bf16[4,1024,1,256]{3,1,2,0:T(8,128)(2,1)}), bf16[4,1024,1,256]{3,1,2,0:T(8,128)(2,1)S(1)}, u32[]{:S(2)}, u32[]{:S(2)}) async-start(bf16[4,1024,1,256]{3,1,2,0:T(8,128)(2,1)} %bitcast.226), calls=%async_computation.1 | async-start | bytes 4194304 | tf_op jit(solution)/shard_map/all_to_all | solution.py:290
  28.9 71.3 %all-gather.10.cloned.1.call-start = ((), (), s32[]{:S(2)}) async-start(), calls=%async_computation.20 | async-start | bytes 1310720 | tf_op jit(solution)/shard_map/all_gather | solution.py:307
  29.6 91.8 %all-gather.14.cloned.1.call-start = ((), (), s32[]{:S(2)}) async-start(), calls=%async_computation.22 | async-start | bytes 1179648 | tf_op jit(solution)/shard_map/all_gather | solution.py:311
  98.5 345.0 %copy-start.8 = (bf16[1,1024,4,1,256]{1,4,2,3,0:T(8,128)(2,1)}, bf16[1,1024,4,1,256]{1,4,2,3,0:T(8,128)(2,1)S(1)}, u32[]{:S(2)}) copy-start(bf16[1,1024,4,1,256]{1,4,2,3,0:T(8,128)(2,1)S(1)} %copy.197) | copy-start | bytes 6291460
  98.6 62.1 %all-gather.22.cloned.1.call-start = ((), (), s32[]{:S(2)}) async-start(), calls=%async_computation.26 | async-start | bytes 1966080 | tf_op jit(solution)/shard_map/all_gather | solution.py:307
  99.6 127.0 %all-gather.18.cloned.1.call-start = ((), (), s32[]{:S(2)}) async-start(), calls=%async_computation.24 | async-start | bytes 1769472 | tf_op jit(solution)/shard_map/all_gather | solution.py:311
  100.1 143.2 %all-gather.12.cloned.1.call-start = ((), (), s32[]{:S(2)}) async-start(), calls=%async_computation.21 | async-start | bytes 9437184 | tf_op jit(solution)/shard_map/all_gather | solution.py:308
  100.7 338.4 %all-gather.16.cloned.1.call-start = ((), (), s32[]{:S(2)}) async-start(), calls=%async_computation.23 | async-start | bytes 5242880 | tf_op jit(solution)/shard_map/all_gather | solution.py:312
  121.4 332.4 %all-gather.24.cloned.1.call-start = ((), (), s32[]{:S(2)}) async-start(), calls=%async_computation.27 | async-start | bytes 14155776 | tf_op jit(solution)/shard_map/all_gather | solution.py:308
  162.4 10.8 %copy-start.31 = (s32[1,4096]{1,0:T(1,128)S(1)}, s32[1,4096]{1,0:T(1,128)}, u32[]{:S(2)}) copy-start(s32[1,4096]{1,0:T(1,128)} %param.22) | copy-start | bytes 49156
  168.7 53.3 %all-to-all-start.4 = ((bf16[4,1024,1,256]{3,1,2,0:T(8,128)(2,1)}), bf16[4,1024,1,256]{3,1,2,0:T(8,128)(2,1)}, u32[]{:S(2)}, u32[]{:S(2)}) async-start(bf16[4,1024,1,256]{3,1,2,0:T(8,128)(2,1)} %bitcast.223), calls=%async_computation.4 | async-start | bytes 4194304 | tf_op jit(solution)/shard_map/all_to_all | solution.py:290
  173.2 342.0 %all-gather.20.cloned.1.call-start = ((), (), s32[]{:S(2)}) async-start(), calls=%async_computation.25 | async-start | bytes 7864320 | tf_op jit(solution)/shard_map/all_gather | solution.py:312
  178.2 65.1 %copy-start.41 = (f32[1024]{0:T(1024)S(1)}, f32[1024]{0:T(1024)}, u32[]{:S(2)}) copy-start(f32[1024]{0:T(1024)} %param.18) | copy-start | bytes 12292
  179.2 176.0 %copy-start.18 = (f32[1024,64]{0,1:T(8,128)}, f32[1024,64]{0,1:T(8,128)S(1)}, u32[]{:S(2)}) copy-start(f32[1024,64]{0,1:T(8,128)S(1)} %get-tuple-element.151) | copy-start | bytes 786436
  179.2 176.0 %copy-start.20 = (f32[1024,64]{0,1:T(8,128)}, f32[1024,64]{0,1:T(8,128)S(1)}, u32[]{:S(2)}) copy-start(f32[1024,64]{0,1:T(8,128)S(1)} %get-tuple-element.152) | copy-start | bytes 786436
  226.5 31.9 %copy-start.33 = (f32[1024]{0:T(1024)}, f32[1024]{0:T(1024)S(1)}, u32[]{:S(2)}) copy-start(f32[1024]{0:T(1024)S(1)} %add_rsqrt_fusion.1) | copy-start | bytes 12292
  278.9 19.5 %copy-start.4 = (f32[1024,8,4,128]{3,2,1,0:T(4,128)S(1)}, f32[1024,8,4,128]{3,2,1,0:T(4,128)}, u32[]{:S(2)}) copy-start(f32[1024,8,4,128]{3,2,1,0:T(4,128)} %reshape.322) | copy-start | bytes 50331652
  317.4 29.5 %copy-start.26 = (f32[1024,8]{0,1:T(8,128)}, f32[1024,8]{0,1:T(8,128)S(1)}, u32[]{:S(2)}) copy-start(f32[1024,8]{0,1:T(8,128)S(1)} %fusion.61) | copy-start | bytes 98308
  342.0 5.4 copy-start.2
  342.0 5.4 copy-start.39
  342.0 8.2 slice-start
  433.4 10.1 all-to-all-start.5
  439.0 315.6 %reduce-scatter.25.cloned.1.call-start = ((), (), s32[]{:S(2)}) async-start(), calls=%async_computation.34 | async-start | bytes 7077888
  443.5 10.3 %copy-start.36 = (f32[1024]{0:T(1024)S(1)}, f32[1024]{0:T(1024)}, u32[]{:S(2)}) copy-start(f32[1024]{0:T(1024)} %param.19) | copy-start | bytes 12292
  453.8 22.6 %copy-start.17 = (bf16[1,1024,4,1,256]{1,4,2,3,0:T(8,128)(2,1)S(1)}, bf16[1,1024,4,1,256]{1,4,2,3,0:T(8,128)(2,1)}, u32[]{:S(2)}) copy-start(bf16[1,1024,4,1,256]{1,4,2,3,0:T(8,128)(2,1)} %copy.208) | copy-start | bytes 6291460
  584.0 172.9 %reduce-scatter.13.cloned.1.call-start = ((), (), s32[]{:S(2)}) async-start(), calls=%async_computation.28 | async-start | bytes 14155776 | tf_op jit(solution)/shard_map/reduce_scatter | solution.py:315
  590.7 6.5 copy-start.5
  590.7 7.9 copy-start.12
  599.9 9.9 copy-start.10
  599.9 9.9 copy-start.45
  648.4 12.4 %all-to-all-start.6 = ((bf16[1,1024,2,1024]{3,1,0,2:T(8,128)(2,1)}), bf16[1,1024,2,1024]{3,1,0,2:T(8,128)(2,1)}, u32[]{:S(2)}, u32[]{:S(2)}) async-start(bf16[1,1024,2,1024]{3,1,0,2:T(8,128)(2,1)} %copy.215), calls=%async_computation.6 | async-start | bytes 8388608 | tf_op jit(solution)/shard_map/all_to_all | solution.py:284
  654.1 176.1 %reduce-scatter.27.cloned.1.call-start = ((), (), s32[]{:S(2)}) async-start(), calls=%async_computation.35 | async-start | bytes 4718592
  660.9 82.2 %all-to-all-start.7 = ((bf16[1,1024,4,256]{1,3,0,2:T(8,128)(2,1)}), bf16[1,1024,4,256]{1,3,0,2:T(8,128)(2,1)S(1)}, u32[]{:S(2)}, u32[]{:S(2)}) async-start(bf16[1,1024,4,256]{1,3,0,2:T(8,128)(2,1)} %bitcast.231), calls=%async_computation.7 | async-start | bytes 4194304 | tf_op jit(solution)/shard_map/all_to_all | solution.py:293
  664.6 237.7 %reduce-scatter.15.cloned.1.call-start = ((), (), s32[]{:S(2)}) async-start(), calls=%async_computation.29 | async-start | bytes 9437184 | tf_op jit(solution)/shard_map/reduce_scatter | solution.py:315
  784.5 9.5 slice-start.2
  809.2 5.9 copy-start.9
  809.2 5.9 copy-start.34
  809.2 5.9 copy-start.42
  830.1 96.8 %reduce-scatter.19.cloned.1.call-start = ((), (), s32[]{:S(2)}) async-start(), calls=%async_computation.31 | async-start | bytes 655360 | tf_op jit(solution)/shard_map/reduce_scatter | solution.py:325
  832.3 144.9 %reduce-scatter.23.cloned.1.call-start = ((), (), s32[]{:S(2)}) async-start(), calls=%async_computation.33 | async-start | bytes 983040 | tf_op jit(solution)/shard_map/reduce_scatter | solution.py:325
  832.9 155.8 %reduce-scatter.21.cloned.1.call-start = ((), (), s32[]{:S(2)}) async-start(), calls=%async_computation.32 | async-start | bytes 1966080 | tf_op jit(solution)/shard_map/reduce_scatter | solution.py:318
  833.4 15.2 %copy-start.11 = (f32[1024,1024]{0,1:T(8,128)S(1)}, f32[1024,1024]{0,1:T(8,128)}, u32[]{:S(2)}) copy-start(f32[1024,1024]{0,1:T(8,128)} %copy-done.10) | copy-start | bytes 12582916
  851.3 77.2 %copy-start.35 = (f32[1024]{0:T(1024)S(1)}, f32[1024]{0:T(1024)}, u32[]{:S(2)}) copy-start(f32[1024]{0:T(1024)} %get-tuple-element.125) | copy-start | bytes 12292
  851.3 118.2 %copy-start.13 = (bf16[2,2,1,1024,256]{4,3,0,1,2:T(8,128)(2,1)S(1)}, bf16[2,2,1,1024,256]{4,3,0,1,2:T(8,128)(2,1)}, u32[]{:S(2)}) copy-start(bf16[2,2,1,1024,256]{4,3,0,1,2:T(8,128)(2,1)} %copy.218) | copy-start | bytes 6291460
  851.3 127.5 %all-to-all-start.10 = ((bf16[1,1024,4,256]{1,3,0,2:T(8,128)(2,1)}), bf16[1,1024,4,256]{1,3,0,2:T(8,128)(2,1)}, u32[]{:S(2)}, u32[]{:S(2)}) async-start(bf16[1,1024,4,256]{1,3,0,2:T(8,128)(2,1)} %bitcast.217), calls=%async_computation.11 | async-start | bytes 4194304 | tf_op jit(solution)/shard_map/all_to_all | solution.py:293
  855.9 161.1 %reduce-scatter.17.cloned.1.call-start = ((), (), s32[]{:S(2)}) async-start(), calls=%async_computation.30 | async-start | bytes 1310720 | tf_op jit(solution)/shard_map/reduce_scatter | solution.py:318
  982.8 8.1 all-to-all-start.11
  (25 other events, 69.5 us)
Sparse Core Ops, SparseCore 0:
  31.2 51.3 all-gather.9
  98.7 22.6 all-gather.13
  123.5 37.0 all-gather.21
  162.4 24.7 all-gather.17
  188.9 54.4 all-gather.11
  244.8 80.7 all-gather.15
  327.5 70.7 all-gather.23
  399.8 115.2 all-gather.19
  584.1 59.9 reduce-scatter.24
  647.9 93.8 reduce-scatter.12
  745.5 51.2 reduce-scatter.26
  830.2 71.9 reduce-scatter.14
  905.2 21.5 reduce-scatter.18
  929.7 21.8 reduce-scatter.22
  953.8 34.7 reduce-scatter.20
  990.9 26.1 reduce-scatter.16
